TPU v7x, 32 devices: a whole 2x2x4 slice. The times are simulated.
32 devices in a mesh: section: 2 (over core), shard: 4 (over z), replica: 4 (over y, x).
Axes of the slice: x: 2, y: 2, z: 4, core: 2. Of those that a mesh axis runs over, the one named last changes fastest.
Arguments:
- edges: bfloat16 [2, 2, 4, 1024, 896], P('section', None, 'replica', 'shard'), may hold values from -6 to 6
- positions: int32 [2, 4, 1024], P(None, 'replica', 'shard'), may hold values from 0 to 767, as said below
- attn_in: bfloat16 [2, 896, 1152], P('section', 'shard'), may hold values from -0.1875 to 0.1875
- out_proj: bfloat16 [2, 896, 896], P('section', 'shard'), may hold values from -1.5 to 1.5
- mlp_in: bfloat16 [2, 896, 9728], P('section', 'shard'), may hold values from -0.1875 to 0.1875
- mlp_out: bfloat16 [2, 4864, 896], P('section', 'shard'), may hold values from -0.078125 to 0.078125
- gains: bfloat16 [2, 1792], P('section', 'shard'), may hold values from 0.5 to 1.5
- bias: bfloat16 [2, 1152], P('section', 'shard'), may hold values from -3 to 3
Outputs:
- layer_outputs: bfloat16 [2, 2, 4, 1024, 896], P('section', None, 'replica', 'shard')
- input_grads: float32 [2, 2, 4, 1024, 896], P('section', None, 'replica', 'shard')
- grad_attn_in: float32 [2, 896, 1152], P('section', 'shard')
- grad_out_proj: float32 [2, 896, 896], P('section', 'shard')
- grad_mlp_in: float32 [2, 896, 9728], P('section', 'shard')
- grad_mlp_out: float32 [2, 4864, 896], P('section', 'shard')
- grad_gains: float32 [2, 1792], P('section', 'shard')
- grad_bias: float32 [2, 1024], P('section', 'shard')
- grad_value_bias: float32 [2, 128], P('section', 'shard')
Inputs may be any that keep to these rules, and one draw needn't show every extreme that they name: In each sequence of 1024 tokens the positions run 0, 1, 2, ... and restart at 0 exactly once, at a token between 256 and 768; in some sequence the restart is at token 768.
All inputs are finite; a program needn't handle non-finite values.
Results may differ from a plain program's by a relative error of at most 0.023.
Values may be sent and summed in bfloat16 or wider, within the bound.
A program may use at most 384 MiB of HBM per device.

v0:
```python
import math

import jax
import jax.numpy as jnp
from jax import lax
from jax.sharding import PartitionSpec as P

D = 896
QUERY_HEADS = 14
KEY_VALUE_HEADS = 2
HEAD_SIZE = 64
FF = 4864
QKV = 1152


eps_norm = 1e-06
rope_base = 1000000.0


def shifted(value, axis, steps):
    count = lax.axis_size(axis)
    leading, last = (max(0, -steps), min(count, count - steps))
    return lax.ppermute(value, axis, [(source, source + steps) for source in range(leading, last)])


def brain_float(values):
    return values.astype(jnp.bfloat16)


def matmul(first_mat, second_mat):
    return jnp.dot(first_mat, second_mat, preferred_element_type=jnp.float32)


def matmul_left(first_mat, second_mat):
    return lax.dot_general(
        first_mat, second_mat, (((0,), (0,)), ((), ())), preferred_element_type=jnp.float32
    )


def matmul_right(first_mat, second_mat):
    return lax.dot_general(
        first_mat, second_mat, (((1,), (1,)), ((), ())), preferred_element_type=jnp.float32
    )


def rotary_tables(token_pos):
    half_dim = HEAD_SIZE // 2
    frequency = jnp.power(rope_base, -2.0 * jnp.arange(half_dim, dtype=jnp.float32) / HEAD_SIZE)
    angles = token_pos.astype(jnp.float32)[:, None] * frequency[None, :]
    return (jnp.cos(angles)[:, None, :], jnp.sin(angles)[:, None, :])


def rotary_embed(values, cosine_table, sine_values):
    half_dim = values.shape[-1] // 2
    first_half = values[..., :half_dim]
    second_half = values[..., half_dim:]
    return jnp.concatenate(
        [
            first_half * cosine_table - second_half * sine_values,
            second_half * cosine_table + first_half * sine_values,
        ],
        axis=-1,
    )


def rotary_backward(grads, cosine_table, sine_values):
    half_dim = grads.shape[-1] // 2
    first_half = grads[..., :half_dim]
    second_half = grads[..., half_dim:]
    return jnp.concatenate(
        [
            first_half * cosine_table + second_half * sine_values,
            second_half * cosine_table - first_half * sine_values,
        ],
        axis=-1,
    )


def visible(token_pos, row_index, seq_len):
    columns = jnp.arange(seq_len, dtype=jnp.int32)
    return (columns[None, :] <= row_index[:, None]) & (
        columns[None, :] >= (row_index - token_pos)[:, None]
    )


def when_active(active, function, operands):

    def skipped(*inner):
        return jax.tree.map(jnp.zeros_like, function(*inner))

    return lax.cond(active, function, skipped, *operands)


def attention_inputs(block_in, token_pos, weights):
    attn_full, out_full, mlp_full, down_full, gain_full, bias_full = weights
    count_of_rows = block_in.shape[0]
    hidden = block_in.astype(jnp.float32)
    inverse = lax.rsqrt(jnp.mean(hidden * hidden, axis=-1, keepdims=True) + eps_norm)
    normed = brain_float(hidden * inverse * gain_full[:D].astype(jnp.float32))
    project_matrix = matmul(normed, attn_full) + bias_full.astype(jnp.float32)
    cosine_table, sine_values = rotary_tables(token_pos)
    query_rows = brain_float(
        rotary_embed(
            project_matrix[:, : QUERY_HEADS * HEAD_SIZE].reshape(
                count_of_rows, QUERY_HEADS, HEAD_SIZE
            ),
            cosine_table,
            sine_values,
        )
    ).reshape(count_of_rows, QUERY_HEADS * HEAD_SIZE)
    keys_here = brain_float(
        rotary_embed(
            project_matrix[
                :, QUERY_HEADS * HEAD_SIZE : (QUERY_HEADS + KEY_VALUE_HEADS) * HEAD_SIZE
            ].reshape(count_of_rows, KEY_VALUE_HEADS, HEAD_SIZE),
            cosine_table,
            sine_values,
        )
    ).reshape(count_of_rows, KEY_VALUE_HEADS * HEAD_SIZE)
    value_rows_local = brain_float(project_matrix[:, (QUERY_HEADS + KEY_VALUE_HEADS) * HEAD_SIZE :])
    return (normed, inverse, query_rows, keys_here, value_rows_local)


def attention_forward(query_rows, keys_all, value_rows_every, allowed):
    count_of_rows = query_rows.shape[0]
    heads_per_group = QUERY_HEADS // KEY_VALUE_HEADS
    scaling = 1.0 / math.sqrt(HEAD_SIZE)
    grouped_heads = query_rows.reshape(count_of_rows, KEY_VALUE_HEADS, heads_per_group, HEAD_SIZE)
    outputs = []
    logsums = []
    for head_cluster in range(KEY_VALUE_HEADS):
        keys_group = keys_all[:, head_cluster * HEAD_SIZE : (head_cluster + 1) * HEAD_SIZE]
        values_group = value_rows_every[
            :, head_cluster * HEAD_SIZE : (head_cluster + 1) * HEAD_SIZE
        ]
        scores = (
            jnp.einsum(
                "ikd,jd->kij",
                grouped_heads[:, head_cluster],
                keys_group,
                preferred_element_type=jnp.float32,
            )
            * scaling
        )
        masked = jnp.where(allowed[None], scores, -1e30)
        row_max = jnp.max(masked, axis=-1, keepdims=True)
        exponent = jnp.exp(masked - row_max)
        row_sum = jnp.sum(exponent, axis=-1, keepdims=True)
        probability = brain_float(exponent / row_sum)
        outputs.append(
            jnp.einsum("kij,jd->ikd", probability, values_group, preferred_element_type=jnp.float32)
        )
        logsums.append((row_max + jnp.log(row_sum))[..., 0])
    return (
        jnp.stack(outputs, axis=1).reshape(count_of_rows, QUERY_HEADS * HEAD_SIZE),
        jnp.stack(logsums, axis=0),
    )


def attention_backward(query_rows, keys_all, value_rows_every, logsum, attended_gradient, allowed):
    count_of_rows = query_rows.shape[0]
    heads_per_group = QUERY_HEADS // KEY_VALUE_HEADS
    scaling = 1.0 / math.sqrt(HEAD_SIZE)
    grouped_heads = query_rows.reshape(count_of_rows, KEY_VALUE_HEADS, heads_per_group, HEAD_SIZE)
    grouped_gradient = attended_gradient.reshape(
        count_of_rows, KEY_VALUE_HEADS, heads_per_group, HEAD_SIZE
    )
    query_parts = []
    key_parts = []
    value_parts = []
    for head_cluster in range(KEY_VALUE_HEADS):
        keys_group = keys_all[:, head_cluster * HEAD_SIZE : (head_cluster + 1) * HEAD_SIZE]
        values_group = value_rows_every[
            :, head_cluster * HEAD_SIZE : (head_cluster + 1) * HEAD_SIZE
        ]
        scores = (
            jnp.einsum(
                "ikd,jd->kij",
                grouped_heads[:, head_cluster],
                keys_group,
                preferred_element_type=jnp.float32,
            )
            * scaling
        )
        masked = jnp.where(allowed[None], scores, -1e30)
        probability = jnp.exp(masked - logsum[head_cluster][..., None])
        value_parts.append(
            jnp.einsum(
                "kij,ikd->jd",
                brain_float(probability),
                grouped_gradient[:, head_cluster],
                preferred_element_type=jnp.float32,
            )
        )
        prob_grad = jnp.einsum(
            "ikd,jd->kij",
            grouped_gradient[:, head_cluster],
            values_group,
            preferred_element_type=jnp.float32,
        )
        inner_sum = jnp.sum(probability * prob_grad, axis=-1, keepdims=True)
        score_low = brain_float(probability * (prob_grad - inner_sum))
        query_parts.append(
            jnp.einsum("kij,jd->ikd", score_low, keys_group, preferred_element_type=jnp.float32)
            * scaling
        )
        key_parts.append(
            jnp.einsum(
                "kij,ikd->jd",
                score_low,
                grouped_heads[:, head_cluster],
                preferred_element_type=jnp.float32,
            )
            * scaling
        )
    return (
        jnp.stack(query_parts, axis=1).reshape(count_of_rows, QUERY_HEADS * HEAD_SIZE),
        jnp.concatenate(key_parts, axis=1),
        jnp.concatenate(value_parts, axis=1),
    )


def finish_forward(block_in, token_pos, row_index, first_part, keys_all, value_rows_every, weights):
    attn_full, out_full, mlp_full, down_full, gain_full, bias_full = weights
    normed, inverse, query_rows, keys_here, value_rows_local = first_part
    allowed = visible(token_pos, row_index, keys_all.shape[0])
    attended, logsum = attention_forward(query_rows, keys_all, value_rows_every, allowed)
    attended_low = brain_float(attended)
    middle = block_in.astype(jnp.float32) + matmul(attended_low, out_full)
    inverse_two = lax.rsqrt(jnp.mean(middle * middle, axis=-1, keepdims=True) + eps_norm)
    normed_two = brain_float(middle * inverse_two * gain_full[D:].astype(jnp.float32))
    gate_up = matmul(normed_two, mlp_full)
    activated = brain_float(jax.nn.silu(gate_up[:, :FF]) * gate_up[:, FF:])
    result = brain_float(middle + matmul(activated, down_full))
    return (result, logsum, attended_low, middle, inverse_two, normed_two, gate_up, activated)


def backward_branches(cotangent, saved_now, row_index, weights):
    attn_full, out_full, mlp_full, down_full, gain_full, bias_full = weights
    block_in, token_pos, first_part, keys_all, value_rows_every, second_part = saved_now
    normed, inverse, query_rows, keys_here, value_rows_local = first_part
    result, logsum, attended_low, middle, inverse_two, normed_two, gate_up, activated = second_part
    mid_grad = matmul_right(cotangent, down_full)
    gate_in = gate_up[:, :FF]
    upward = gate_up[:, FF:]
    sigmoid_g = jax.nn.sigmoid(gate_in)
    gate_grad = mid_grad * upward * sigmoid_g * (1.0 + gate_in * (1.0 - sigmoid_g))
    up_grad = mid_grad * gate_in * sigmoid_g
    gate_up_low = brain_float(jnp.concatenate([gate_grad, up_grad], axis=1))
    normed_grad = matmul_right(gate_up_low, mlp_full)
    plain_two = middle * inverse_two
    gain_grad_two = jnp.sum(normed_grad * plain_two, axis=0)
    scaled_two = normed_grad * gain_full[D:].astype(jnp.float32)
    middle_grad = cotangent.astype(jnp.float32) + inverse_two * (
        scaled_two - plain_two * jnp.mean(scaled_two * plain_two, axis=-1, keepdims=True)
    )
    branch_low = brain_float(middle_grad)
    attended_gradient = brain_float(matmul_right(branch_low, out_full))
    allowed = visible(token_pos, row_index, keys_all.shape[0])
    query_grad, key_part, value_part = attention_backward(
        query_rows, keys_all, value_rows_every, logsum, attended_gradient, allowed
    )
    return (query_grad, key_part, value_part, middle_grad, branch_low, gate_up_low, gain_grad_two)


def backward_inputs(back_part, key_gradients, value_grads, saved_now, weights):
    attn_full, out_full, mlp_full, down_full, gain_full, bias_full = weights
    block_in, token_pos, first_part, keys_all, value_rows_every, second_part = saved_now
    normed, inverse, query_rows, keys_here, value_rows_local = first_part
    query_grad, key_part, value_part, middle_grad, branch_low, gate_up_low, gain_grad_two = (
        back_part
    )
    count_of_rows = block_in.shape[0]
    cosine_table, sine_values = rotary_tables(token_pos)
    query_back = rotary_backward(
        query_grad.reshape(count_of_rows, QUERY_HEADS, HEAD_SIZE), cosine_table, sine_values
    ).reshape(count_of_rows, QUERY_HEADS * HEAD_SIZE)
    key_backward = rotary_backward(
        key_gradients.reshape(count_of_rows, KEY_VALUE_HEADS, HEAD_SIZE), cosine_table, sine_values
    ).reshape(count_of_rows, KEY_VALUE_HEADS * HEAD_SIZE)
    project_low = brain_float(jnp.concatenate([query_back, key_backward, value_grads], axis=1))
    bias_grad = jnp.sum(project_low, axis=0, dtype=jnp.float32)
    normed_grad = matmul_right(project_low, attn_full)
    plain_one = block_in.astype(jnp.float32) * inverse
    gain_grad_one = jnp.sum(normed_grad * plain_one, axis=0)
    scaled_one = normed_grad * gain_full[:D].astype(jnp.float32)
    input_grad = middle_grad + inverse * (
        scaled_one - plain_one * jnp.mean(scaled_one * plain_one, axis=-1, keepdims=True)
    )
    return (input_grad, project_low, jnp.concatenate([gain_grad_one, gain_grad_two]), bias_grad)


def local(edges, positions, attn_in, out_proj, mlp_in, mlp_out, gains, bias):
    section_id = lax.axis_index("section")
    shard_id = lax.axis_index("shard")
    shard_count = lax.axis_size("shard")
    micro_count = edges.shape[1]
    count_of_rows = edges.shape[3]
    local_data = edges[0, :, 0]
    all_pos = positions[:, 0]
    row_index = shard_id * count_of_rows + jnp.arange(count_of_rows, dtype=jnp.int32)
    gathered = (
        lax.all_gather(attn_in, "shard", axis=1, tiled=True),
        lax.all_gather(out_proj, "shard", axis=1, tiled=True),
        lax.all_gather(mlp_in, "shard", axis=1, tiled=True),
        lax.all_gather(mlp_out, "shard", axis=1, tiled=True),
        lax.all_gather(gains, "shard", axis=1, tiled=True),
        lax.all_gather(bias, "shard", axis=1, tiled=True),
    )
    forward_weights = tuple((gathered_one[0] for gathered_one in gathered))
    received = jnp.zeros((count_of_rows, D), jnp.bfloat16)
    outputs = []
    saved_all = []
    for moment in range(micro_count + 1):
        micro_id = moment - section_id
        active = (micro_id >= 0) & (micro_id < micro_count)
        chosen = jnp.clip(micro_id, 0, micro_count - 1)
        own_block = lax.dynamic_index_in_dim(local_data, chosen, 0, keepdims=False)
        token_pos = lax.dynamic_index_in_dim(all_pos, chosen, 0, keepdims=False)
        block_in = jnp.where(section_id == 0, own_block, received)
        first_part = when_active(active, attention_inputs, (block_in, token_pos, forward_weights))
        keys_all, value_rows_every = (
            lax.all_gather(first_part[3], "shard", axis=0, tiled=True),
            lax.all_gather(first_part[4], "shard", axis=0, tiled=True),
        )
        second_part = when_active(
            active,
            finish_forward,
            (
                block_in,
                token_pos,
                row_index,
                first_part,
                keys_all,
                value_rows_every,
                forward_weights,
            ),
        )
        outputs.append(second_part[0])
        saved_all.append((block_in, token_pos, first_part, keys_all, value_rows_every, second_part))
        if moment < micro_count:
            received = shifted(second_part[0], "section", 1)
    received_grad = jnp.zeros((count_of_rows, D), jnp.bfloat16)
    grads_out = []
    records = []
    gain_sum = jnp.zeros((2 * D,), jnp.float32)
    bias_sum = jnp.zeros((QKV,), jnp.float32)
    for moment in range(micro_count + 1):
        micro_id = moment - (1 - section_id)
        active = (micro_id >= 0) & (micro_id < micro_count)
        chosen = jnp.clip(micro_id, 0, micro_count - 1)
        own_block = lax.dynamic_index_in_dim(local_data, chosen, 0, keepdims=False)
        cotangent = jnp.where(section_id == 1, own_block, received_grad)
        earlier = saved_all[max(moment - 1, 0)]
        later_one = saved_all[min(moment + 1, micro_count)]
        saved_now = jax.tree.map(
            lambda low_side, high_side: jnp.where(section_id == 0, low_side, high_side),
            earlier,
            later_one,
        )
        back_part = when_active(
            active, backward_branches, (cotangent, saved_now, row_index, forward_weights)
        )
        key_gradients, value_grads = (
            lax.psum_scatter(
                back_part[1].astype(jnp.bfloat16), "shard", scatter_dimension=0, tiled=True
            ).astype(jnp.float32),
            lax.psum_scatter(
                back_part[2].astype(jnp.bfloat16), "shard", scatter_dimension=0, tiled=True
            ).astype(jnp.float32),
        )
        final_part = when_active(
            active,
            backward_inputs,
            (back_part, key_gradients, value_grads, saved_now, forward_weights),
        )
        grads_out.append(final_part[0])
        first_saved = saved_now[2]
        second_saved = saved_now[5]
        records.append(
            (
                first_saved[0],
                final_part[1],
                second_saved[2],
                back_part[4],
                second_saved[5],
                back_part[5],
                second_saved[7],
                cotangent,
            )
        )
        gain_sum = gain_sum + final_part[2]
        bias_sum = bias_sum + final_part[3]
        if moment < micro_count:
            received_grad = shifted(brain_float(final_part[0]), "section", -1)

    def by_micro(series, zero_offset, one_offset):
        return [
            jax.tree.map(
                lambda zero_side, one_side: jnp.where(section_id == 0, zero_side, one_side),
                series[micro_index + zero_offset],
                series[micro_index + one_offset],
            )
            for micro_index in range(micro_count)
        ]

    layer_outputs = jnp.stack(by_micro(outputs, 0, 1), axis=0)[None, :, None]
    input_grads = jnp.stack(by_micro(grads_out, 1, 0), axis=0)[None, :, None]
    chosen_records = by_micro(records, 1, 0)
    joined = tuple(
        (
            jnp.concatenate([record_one[field_id] for record_one in chosen_records], axis=0)
            for field_id in range(8)
        )
    )
    grad_attn = matmul_left(joined[0], joined[1])
    grad_out = matmul_left(joined[2], joined[3])
    grad_mlp = matmul_left(joined[4], joined[5])
    grad_down = matmul_left(joined[6], joined[7])
    query_key = (QUERY_HEADS + KEY_VALUE_HEADS) * HEAD_SIZE
    value_width = KEY_VALUE_HEADS * HEAD_SIZE
    arranged = jnp.concatenate(
        [
            bias_sum[:query_key].reshape(shard_count, query_key // shard_count),
            bias_sum[query_key:].reshape(shard_count, value_width // shard_count),
        ],
        axis=1,
    ).reshape(QKV)
    summed = (
        lax.psum_scatter(
            grad_attn.astype(jnp.bfloat16), "shard", scatter_dimension=0, tiled=True
        ).astype(jnp.float32),
        lax.psum_scatter(
            grad_out.astype(jnp.bfloat16), "shard", scatter_dimension=0, tiled=True
        ).astype(jnp.float32),
        lax.psum_scatter(
            grad_mlp.astype(jnp.bfloat16), "shard", scatter_dimension=0, tiled=True
        ).astype(jnp.float32),
        lax.psum_scatter(
            grad_down.astype(jnp.bfloat16), "shard", scatter_dimension=0, tiled=True
        ).astype(jnp.float32),
        lax.psum_scatter(
            gain_sum.astype(jnp.bfloat16), "shard", scatter_dimension=0, tiled=True
        ).astype(jnp.float32),
        lax.psum_scatter(
            arranged.astype(jnp.bfloat16), "shard", scatter_dimension=0, tiled=True
        ).astype(jnp.float32),
    )
    totals = (
        lax.psum(summed[0].astype(jnp.bfloat16), "replica").astype(jnp.float32),
        lax.psum(summed[1].astype(jnp.bfloat16), "replica").astype(jnp.float32),
        lax.psum(summed[2].astype(jnp.bfloat16), "replica").astype(jnp.float32),
        lax.psum(summed[3].astype(jnp.bfloat16), "replica").astype(jnp.float32),
        lax.psum(summed[4].astype(jnp.bfloat16), "replica").astype(jnp.float32),
        lax.psum(summed[5].astype(jnp.bfloat16), "replica").astype(jnp.float32),
    )
    bias_block = totals[5]
    query_key_part = bias_block[: query_key // shard_count]
    value_part = bias_block[query_key // shard_count :]
    return (
        layer_outputs,
        input_grads,
        totals[0][None],
        totals[1][None],
        totals[2][None],
        totals[3][None],
        totals[4][None],
        query_key_part[None],
        value_part[None],
    )


def solution(mesh):
    return jax.shard_map(
        local,
        mesh=mesh,
        in_specs=(
            P("section", None, "replica", "shard", None),
            P(None, "replica", "shard"),
            P("section", "shard", None),
            P("section", "shard", None),
            P("section", "shard", None),
            P("section", "shard", None),
            P("section", "shard"),
            P("section", "shard"),
        ),
        out_specs=(
            P("section", None, "replica", "shard", None),
            P("section", None, "replica", "shard", None),
            P("section", "shard", None),
            P("section", "shard", None),
            P("section", "shard", None),
            P("section", "shard", None),
            P("section", "shard"),
            P("section", "shard"),
            P("section", "shard"),
        ),
        check_vma=False,
    )
```

profile of v0, /device:TPU:0, one launch (start us, length us, event | category | flops | bytes accessed | tf_op | source)
XLA Modules:
  0.0 1967.5 jit_solution(2523890605822194092)
XLA Ops:
  27.8 30.0 %all-gather.5.cloned.1.call-done = bf16[1,896,1152]{2,1,0:T(8,128)(2,1)} async-done(((bf16[1,224,1152]{2,1,0:T(8,128)(2,1)}), bf16[1,896,1152]{2,1,0:T(8,128)(2,1)}) %all-gather.5.cloned.1.call-update) | async-done | bytes 2064400 | tf_op jit(solution)/shard_map/all_gather | solution.py:303
  66.7 16.2 all_gather.39
  82.9 15.9 all_gather.40
  101.6 156.7 %all-gather.11.cloned.1.call-done = bf16[1,4864,896]{2,1,0:T(8,128)(2,1)} async-done(((bf16[1,1216,896]{2,1,0:T(8,128)(2,1)}), bf16[1,4864,896]{2,1,0:T(8,128)(2,1)}) %all-gather.11.cloned.1.call-update) | async-done | bytes 8716304 | tf_op jit(solution)/shard_map/all_gather | solution.py:306
  258.3 298.8 %all-gather.9.cloned.1.call-done = bf16[1,896,9728]{2,1,0:T(8,128)(2,1)} async-done(((bf16[1,224,9728]{2,1,0:T(8,128)(2,1)}), bf16[1,896,9728]{2,1,0:T(8,128)(2,1)}) %all-gather.9.cloned.1.call-update) | async-done | bytes 17432592 | tf_op jit(solution)/shard_map/all_gather | solution.py:305
  557.0 41.0 %conditional.13 = (bf16[256,896]{1,0:T(8,128)(2,1)S(1)}, f32[2,7,256]{2,1,0:T(8,128)S(1)}, f32[256,896]{1,0:T(8,128)}, f32[256,1]{0,1:T(1,128)}, bf16[256,896]{1...) conditional(s32[]{:T(128)} %convert_element_type.372, ...), branch_computations={%region_3.4_spmd, %region_4.10_spmd} | conditional | flops 8099497472 | bytes 117119944 | solution.py:91
  613.4 14.1 all_gather.44
  642.2 40.7 %conditional.15 = (bf16[256,896]{1,0:T(8,128)(2,1)S(1)}, f32[2,7,256]{2,1,0:T(8,128)S(1)}, f32[256,896]{1,0:T(8,128)}, f32[256,1]{0,1:T(1,128)}, bf16[256,896]{1...) conditional(s32[]{:T(128)} %convert_element_type.373, ...), branch_computations={%region_13.14_spmd, %region_14.20_spmd} | conditional | flops 8099497472 | bytes 136580032 | solution.py:91
  700.3 94.6 %collective-permute-start.1 = (bf16[256,896]{1,0:T(8,128)(2,1)}, bf16[256,896]{1,0:T(8,128)(2,1)}, u32[]{:S(2)}, u32[]{:S(2)}) collective-permute-start(bf16[256,896]{1,0:T(8,128)(2,1)} %copy-done.55), channel_id=1, source_target_pairs={{0,16},{1,17},{2,18},{3,19},{4,20},{5,21},{6,22},{7,23},{8,24},{9,... | collective-permute-start | bytes 1376264 | tf_op jit(solution)/shard_map/ppermute | solution.py:23
  794.8 14.5 reduce-scatter.11.cloned.1.call-done
  810.9 19.2 reduce-scatter.13.cloned.1.call-done
  863.4 14.5 all_gather.47
  892.9 114.8 %conditional.20 = (f32[256,896]{0,1:T(8,128)}, bf16[1024,128]{0,1:T(8,128)(2,1)}, bf16[1024,128]{0,1:T(8,128)(2,1)}, f32[256,896]{1,0:T(8,128)}, bf16[256,896]{1...) conditional(s32[]{:T(128)} %convert_element_type.375, () %tuple.117, (s32[256]{0:T(256)S(1)}, ...), branch_computations={%region_43.44_spmd, %region_44.49_spmd} | conditional | flops 9544138752 | bytes 288466432 | solution.py:91
  934.2 19.5 multiply_reduce_fusion.7
  1008.5 60.8 %reduce-scatter.15.cloned.1.call-done = bf16[256,128]{0,1:T(8,128)(2,1)} async-done(((bf16[1024,128]{0,1:T(8,128)(2,1)}), bf16[256,128]{0,1:T(8,128)(2,1)}) %reduce-scatter.15.cloned.1.call-update) | async-done | bytes 65552 | tf_op jit(solution)/shard_map/reduce_scatter | solution.py:365
  1070.8 18.7 reduce-scatter.17.cloned.1.call-done
  1108.2 109.9 %conditional.22 = (f32[256,896]{0,1:T(8,128)}, bf16[1024,128]{0,1:T(8,128)(2,1)}, bf16[1024,128]{0,1:T(8,128)(2,1)}, f32[256,896]{1,0:T(8,128)}, bf16[256,896]{1...) conditional(s32[]{:T(128)} %convert_element_type.386, () %tuple.125, (s32[256]{0:T(256)S(1)}, ...), branch_computations={%region_56.57_spmd, %region_57.62_spmd} | conditional | flops 9544138752 | bytes 292923872 | solution.py:91
  1147.7 19.7 %multiply_reduce_fusion.11 = (f32[896]{0:T(1024)}, f32[256]{0:T(256)S(1)}, f32[256,896]{1,0:T(8,128)}, f32[256,896]{1,0:T(8,128)}) fusion(f32[896]{0:T(1024)S(1)} %slice_convert_fusion.13, f32[256]{0:T(256)S(1)} %bitcast.763, pred[256,896]{1,0:T(32,128)(4,1)S(1)} %copy-done.34, f32[256,896]{1,0:T(8,128)} %get-tuple-element.515, ...), kind=kOutput, calls=%fused_computation.422 | convolution fusion | flops 4464344064 | bytes 26321920 | tf_op jit(solution)/shard_map/cond/branch_1_fun/dot_general | solution.py:41
  1237.1 19.2 reduce-scatter.21.cloned.1.call-done
  1291.1 15.3 convolution_convert_fusion.3
  1306.6 31.7 %reduce-scatter.23.cloned.1.call-done = bf16[224,1152]{1,0:T(8,128)(2,1)} async-done(((bf16[896,1152]{1,0:T(8,128)(2,1)}), bf16[224,1152]{1,0:T(8,128)(2,1)}) %reduce-scatter.23.cloned.1.call-update) | async-done | bytes 516112 | tf_op jit(solution)/shard_map/reduce_scatter | solution.py:430
  1338.3 152.1 %reduce-scatter.29.cloned.1.call-done = bf16[1216,896]{1,0:T(8,128)(2,1)} async-done(((bf16[4864,896]{1,0:T(8,128)(2,1)}), bf16[1216,896]{1,0:T(8,128)(2,1)}) %reduce-scatter.29.cloned.1.call-update) | async-done | bytes 2179088 | tf_op jit(solution)/shard_map/reduce_scatter | solution.py:439
  1490.4 293.9 %reduce-scatter.27.cloned.1.call-done = bf16[224,9728]{1,0:T(8,128)(2,1)} async-done(((bf16[896,9728]{1,0:T(8,128)(2,1)}), bf16[224,9728]{1,0:T(8,128)(2,1)}) %reduce-scatter.27.cloned.1.call-update) | async-done | bytes 4358160 | tf_op jit(solution)/shard_map/reduce_scatter | solution.py:436
  1813.1 135.1 %all-reduce.10.cloned.1.call-done = (bf16[1,224,1152]{2,1,0:T(8,128)(2,1)}, bf16[1,224,896]{2,1,0:T(8,128)(2,1)}, bf16[1,224,9728]{2,1,0:T(8,128)(2,1)}, bf16[1,1216,896]{2,1,0:T(8,128)(2,1)}) async-done(((bf16[1,224,1152]{2,1,0:T(8,128)(2,1)}, bf16[1,224,896]{2,1,0:T(8,128)(2,1)}, bf16[1,224,9728]{2,1,0:T(8,128)(2,1)}, bf16[1,1216,896]{2,1,0:T(8,128)(2,1)}), (bf16[1,224,1152]{2,1,0:T(8,128)(2,1)}, ...) | async-done | bytes 7454736 | tf_op jit(solution)/shard_map/psum | solution.py:450
  (501 shorter events, 569.5 us)
Async XLA Ops:
  7.2 50.6 %all-gather.5.cloned.1.call-start = ((), (), s32[]{:S(2)}) async-start(), calls=%async_computation.10 | async-start | bytes 2580480 | tf_op jit(solution)/shard_map/all_gather | solution.py:303
  8.0 93.6 %all-gather.7.cloned.1.call-start = ((), (), s32[]{:S(2)}) async-start(), calls=%async_computation.11 | async-start | bytes 2007040 | tf_op jit(solution)/shard_map/all_gather | solution.py:304
  8.7 249.6 %all-gather.11.cloned.1.call-start = ((), (), s32[]{:S(2)}) async-start(), calls=%async_computation.13 | async-start | bytes 10895360 | tf_op jit(solution)/shard_map/all_gather | solution.py:306
  9.4 547.6 %all-gather.9.cloned.1.call-start = ((), (), s32[]{:S(2)}) async-start(), calls=%async_computation.12 | async-start | bytes 21790720 | tf_op jit(solution)/shard_map/all_gather | solution.py:305
  10.0 799.3 %reduce-scatter.11.cloned.1.call-start = ((), (), s32[]{:S(2)}) async-start(), calls=%async_computation.14 | async-start | bytes 327680 | tf_op jit(solution)/shard_map/reduce_scatter | solution.py:365
  26.3 574.6 %copy-start.81 = (bf16[1152]{0:T(1024)(128)(2,1)}, bf16[1152]{0:T(1024)(128)(2,1)S(1)}, u32[]{:S(2)}) copy-start(bf16[1152]{0:T(1024)(128)(2,1)S(1)} %get-tuple-element.1197) | copy-start | bytes 6916
  26.9 572.5 %copy-start.91 = (s32[1,1,256]{2,1,0:T(1,128)}, s32[1,1,256]{2,1,0:T(1,128)S(1)}, u32[]{:S(2)}) copy-start(s32[1,1,256]{2,1,0:T(1,128)S(1)} %get-tuple-element.1337) | copy-start | bytes 3076
  27.8 529.2 %copy-start.12 = (bf16[256,896]{1,0:T(8,128)(2,1)}, bf16[256,896]{1,0:T(8,128)(2,1)S(1)}, u32[]{:S(2)}) copy-start(bf16[256,896]{1,0:T(8,128)(2,1)S(1)} %get-tuple-element.1330) | copy-start | bytes 1376260
  598.1 2.7 collective-permute-start
  699.7 130.4 %reduce-scatter.13.cloned.1.call-start = ((), (), s32[]{:S(2)}) async-start(), calls=%async_computation.15 | async-start | bytes 327680 | tf_op jit(solution)/shard_map/reduce_scatter | solution.py:368
  700.2 369.0 %reduce-scatter.15.cloned.1.call-start = ((), (), s32[]{:S(2)}) async-start(), calls=%async_computation.16 | async-start | bytes 327680 | tf_op jit(solution)/shard_map/reduce_scatter | solution.py:365
  700.3 133.8 %collective-permute-start.1 = (bf16[256,896]{1,0:T(8,128)(2,1)}, bf16[256,896]{1,0:T(8,128)(2,1)}, u32[]{:S(2)}, u32[]{:S(2)}) collective-permute-start(bf16[256,896]{1,0:T(8,128)(2,1)} %copy-done.55), channel_id=1, source_target_pairs={{0,16},{1,17},{2,18},{3,19},{4,20},{5,21},{6,22},{7,23},{8,24},{9,... | collective-permute-start | bytes 1376264 | tf_op jit(solution)/shard_map/ppermute | solution.py:23
  832.8 11.1 collective-permute-start.2
  1007.7 81.8 %reduce-scatter.17.cloned.1.call-start = ((), (), s32[]{:S(2)}) async-start(), calls=%async_computation.17 | async-start | bytes 327680 | tf_op jit(solution)/shard_map/reduce_scatter | solution.py:368
  1008.4 227.9 %reduce-scatter.19.cloned.1.call-start = ((), (), s32[]{:S(2)}) async-start(), calls=%async_computation.18 | async-start | bytes 327680 | tf_op jit(solution)/shard_map/reduce_scatter | solution.py:365
  1102.1 4.0 collective-permute-start.3
  1218.1 38.2 %reduce-scatter.21.cloned.1.call-start = ((), (), s32[]{:S(2)}) async-start(), calls=%async_computation.19 | async-start | bytes 327680 | tf_op jit(solution)/shard_map/reduce_scatter | solution.py:368
  1218.7 87.9 %reduce-scatter.25.cloned.1.call-start = ((), (), s32[]{:S(2)}) async-start(), calls=%async_computation.21 | async-start | bytes 2007040 | tf_op jit(solution)/shard_map/reduce_scatter | solution.py:433
  1225.0 113.3 %reduce-scatter.23.cloned.1.call-start = ((), (), s32[]{:S(2)}) async-start(), calls=%async_computation.20 | async-start | bytes 2580480 | tf_op jit(solution)/shard_map/reduce_scatter | solution.py:430
  1270.7 219.7 %reduce-scatter.29.cloned.1.call-start = ((), (), s32[]{:S(2)}) async-start(), calls=%async_computation.23 | async-start | bytes 10895360 | tf_op jit(solution)/shard_map/reduce_scatter | solution.py:439
  1282.2 502.0 %reduce-scatter.27.cloned.1.call-start = ((), (), s32[]{:S(2)}) async-start(), calls=%async_computation.22 | async-start | bytes 21790720 | tf_op jit(solution)/shard_map/reduce_scatter | solution.py:436
  1306.5 504.5 %copy-start.7 = (f32[256,896]{1,0:T(8,128)S(1)}, f32[256,896]{1,0:T(8,128)}, u32[]{:S(2)}) copy-start(f32[256,896]{1,0:T(8,128)} %copy-done.6) | copy-start | bytes 2752516
  1306.5 504.5 %copy-start.9 = (f32[256,896]{1,0:T(8,128)S(1)}, f32[256,896]{1,0:T(8,128)}, u32[]{:S(2)}) copy-start(f32[256,896]{1,0:T(8,128)} %copy-done.8) | copy-start | bytes 2752516
  1306.6 641.6 %all-reduce.10.cloned.1.call-start = ((), (), s32[]{:S(2)}) async-start(), calls=%async_computation.24 | async-start | bytes 14909440 | tf_op jit(solution)/shard_map/psum | solution.py:450
  (95 other events, 5097.0 us)
Sparse Core Ops, SparseCore 0:
  9.6 48.1 all-gather.4
  59.4 42.1 all-gather.6
  103.1 155.0 all-gather.10
  259.7 297.2 all-gather.8
  699.8 109.5 reduce-scatter.10
  812.1 17.8 reduce-scatter.12
  1007.8 61.4 reduce-scatter.14
  1071.6 17.7 reduce-scatter.16
  1218.3 17.9 reduce-scatter.18
  1238.5 17.8 reduce-scatter.20
  1259.3 34.0 reduce-scatter.24
  1296.1 42.1 reduce-scatter.22
  1341.4 148.9 reduce-scatter.28
  1492.6 291.5 reduce-scatter.26
  1788.3 159.7 all-reduce.9
where the time goes:
time: 1980 us; the launch traced here: 1970 us
  waiting for transfers between devices  1260 us (64%)
  matrix products  238 us (12%)
  other arithmetic  158 us (8%)
  blocking collectives  124 us (6%)
  starting transfers between devices  99.2 us (5%)
  local copies, waits for them, and re-layouts  58.7 us (3%)
    all_gather x1, waiting for transfers between devices, local(): lax.all_gather(mlp_in, 'shard', axis=1, tiled=True)  299 us
    reduce_scatter x1, waiting for transfers between devices, local(): lax.psum_scatter(grad_mlp.astype(jnp.bfloat16), 'shard', scatter_dimensio...  294 us
    all_gather x1, waiting for transfers between devices, local(): lax.all_gather(mlp_out, 'shard', axis=1, tiled=True)  157 us
    reduce_scatter x1, waiting for transfers between devices, local(): lax.psum_scatter(grad_down.astype(jnp.bfloat16), 'shard', scatter_dimensi...  152 us
    psum x1, waiting for transfers between devices, local(): lax.psum(summed[0].astype(jnp.bfloat16), 'replica').astype(jnp.float32)  135 us
    ppermute x4, starting transfers between devices, shifted(): lax.ppermute(value, axis, [(source, source + steps) for source in range(l...  98.4 us
    reduce_scatter x3, waiting for transfers between devices, local(): lax.psum_scatter(back_part[1].astype(jnp.bfloat16), 'shard', scatter_dime...  84.4 us
    dot_general x8, matrix products, matmul_right(): lax.dot_general(first_mat, second_mat, (((1,), (1,)), ((), ())), preferre...  64.1 us
  transfers between devices with their start and end apart: 19, of which 17 were waited for; matrix products, arithmetic and copies ran while one was open for 4% of the time, Pallas kernels for 0%

commit v1 on v0

--- a/solution.py
+++ b/solution.py
@@ -3,6 +3,8 @@
 import jax
 import jax.numpy as jnp
 from jax import lax
+from jax.experimental import pallas as pl
+from jax.experimental.pallas import tpu as pltpu
 from jax.sharding import PartitionSpec as P
 
 D = 896
@@ -15,12 +17,6 @@
 
 eps_norm = 1e-06
 rope_base = 1000000.0
-
-
-def shifted(value, axis, steps):
-    count = lax.axis_size(axis)
-    leading, last = (max(0, -steps), min(count, count - steps))
-    return lax.ppermute(value, axis, [(source, source + steps) for source in range(leading, last)])
 
 
 def brain_float(values):
@@ -81,14 +77,6 @@
     return (columns[None, :] <= row_index[:, None]) & (
         columns[None, :] >= (row_index - token_pos)[:, None]
     )
-
-
-def when_active(active, function, operands):
-
-    def skipped(*inner):
-        return jax.tree.map(jnp.zeros_like, function(*inner))
-
-    return lax.cond(active, function, skipped, *operands)
 
 
 def attention_inputs(block_in, token_pos, weights):
@@ -235,10 +223,9 @@
     return (result, logsum, attended_low, middle, inverse_two, normed_two, gate_up, activated)
 
 
-def backward_branches(cotangent, saved_now, row_index, weights):
+def backward_mlp(cotangent, saved_now, weights):
     attn_full, out_full, mlp_full, down_full, gain_full, bias_full = weights
-    block_in, token_pos, first_part, keys_all, value_rows_every, second_part = saved_now
-    normed, inverse, query_rows, keys_here, value_rows_local = first_part
+    second_part = saved_now[5]
     result, logsum, attended_low, middle, inverse_two, normed_two, gate_up, activated = second_part
     mid_grad = matmul_right(cotangent, down_full)
     gate_in = gate_up[:, :FF]
@@ -248,6 +235,15 @@
     up_grad = mid_grad * gate_in * sigmoid_g
     gate_up_low = brain_float(jnp.concatenate([gate_grad, up_grad], axis=1))
     normed_grad = matmul_right(gate_up_low, mlp_full)
+    return (gate_up_low, normed_grad)
+
+
+def backward_branches(cotangent, mlp_part, saved_now, row_index, weights):
+    attn_full, out_full, mlp_full, down_full, gain_full, bias_full = weights
+    block_in, token_pos, first_part, keys_all, value_rows_every, second_part = saved_now
+    normed, inverse, query_rows, keys_here, value_rows_local = first_part
+    result, logsum, attended_low, middle, inverse_two, normed_two, gate_up, activated = second_part
+    gate_up_low, normed_grad = mlp_part
     plain_two = middle * inverse_two
     gain_grad_two = jnp.sum(normed_grad * plain_two, axis=0)
     scaled_two = normed_grad * gain_full[D:].astype(jnp.float32)
@@ -290,183 +286,366 @@
     return (input_grad, project_low, jnp.concatenate([gain_grad_one, gain_grad_two]), bias_grad)
 
 
+MESH = pl.DeviceIdType.MESH
+
+
+def gather_kernel(
+    a_in, m_in, o_in, a_out, m_out, o_out, here, zs, zr, rs, rr, ds, dr, own_s, own_r, cs, cr
+):
+    section = lax.axis_index("section")
+    shard = lax.axis_index("shard")
+    replica = lax.axis_index("replica")
+    nz = lax.axis_size("shard")
+    other = 1 - section
+    near = replica + 1 - 2 * lax.rem(replica, 2)
+    far = lax.rem(replica + 2, 4)
+    across = 3 - replica
+    a_cols = a_in.shape[1] // 4
+    m_cols = m_in.shape[2] // 4
+
+    def piece(p, layer, z, q):
+        if p == 0:
+            return a_out.at[layer, z, :, pl.ds(pl.multiple_of(q * a_cols, 128), a_cols)]
+        if p == 3:
+            return o_out.at[layer, z, q]
+        return m_out.at[layer, z, p - 1, :, pl.ds(pl.multiple_of(q * m_cols, 128), m_cols)]
+
+    def source(p, q):
+        if p == 0:
+            return a_in.at[:, pl.ds(pl.multiple_of(q * a_cols, 128), a_cols)]
+        if p == 3:
+            return o_in.at[q]
+        return m_in.at[p - 1, :, pl.ds(pl.multiple_of(q * m_cols, 128), m_cols)]
+
+    def remote(src, dst, send, recv, target):
+        return pltpu.make_async_remote_copy(
+            src_ref=src,
+            dst_ref=dst,
+            send_sem=send,
+            recv_sem=recv,
+            device_id=target,
+            device_id_type=MESH,
+        )
+
+    barrier = pltpu.get_barrier_semaphore()
+    peers = [{"shard": lax.rem(shard + k, nz)} for k in range(1, nz)]
+    peers += [{"replica": near}, {"replica": far}, {"section": other}]
+    for peer in peers:
+        pl.semaphore_signal(barrier, inc=1, device_id=peer, device_id_type=MESH)
+    pl.semaphore_wait(barrier, len(peers))
+
+    order = sorted(range(1, nz), key=lambda k: min(k, nz - k))
+    sent = []
+
+    def along(p, k):
+        return remote(
+            source(p, replica),
+            piece(p, section, shard, replica),
+            zs.at[p, k],
+            zr.at[p, k],
+            {"shard": lax.rem(shard + k, nz)},
+        )
+
+    for p in range(4):
+        for k in order:
+            copy = along(p, k)
+            copy.start()
+            sent.append(copy)
+    wholes = (
+        (a_in, a_out.at[section, shard], a_out.at[other, shard]),
+        (m_in, m_out.at[section, shard], m_out.at[other, shard]),
+        (o_in, o_out.at[section, shard], o_out.at[other, shard]),
+    )
+    locals_here = []
+    arrivals = []
+    for index, (src, dst, landing) in enumerate(wholes):
+        copy = pltpu.make_async_copy(src, dst, here.at[index])
+        copy.start()
+        locals_here.append(copy)
+        copy = remote(src, dst, own_s.at[index], own_r.at[index], {"section": other})
+        copy.start()
+        sent.append(copy)
+        arrivals.append(
+            remote(src, landing, own_s.at[index], own_r.at[index], {"section": other})
+        )
+
+    def to_core(p, k, kind, q):
+        z = lax.rem(shard + nz - k, nz)
+        ref = piece(p, section, z, q)
+        copy = remote(ref, ref, cs.at[kind, p, k], cr.at[kind, p, k], {"section": other})
+        copy.start()
+        sent.append(copy)
+        landing = piece(p, other, z, q)
+        arrivals.append(
+            remote(
+                landing, landing, cs.at[kind, p, k], cr.at[kind, p, k], {"section": other}
+            )
+        )
+
+    def first_hop(p, k):
+        z = lax.rem(shard + nz - k, nz)
+        ref = piece(p, section, z, replica)
+        remote(ref, ref, zs.at[p, k], zr.at[p, k], {"shard": z}).wait_recv()
+        for way, target in enumerate((near, far)):
+            copy = remote(ref, ref, rs.at[way, p, k], rr.at[way, p, k], {"replica": target})
+            copy.start()
+            sent.append(copy)
+        to_core(p, k, 0, replica)
+
+    def second_hop(p, k):
+        z = lax.rem(shard + nz - k, nz)
+        by_near = (p + (k if p in (0, 3) else 0)) % 2 == 0
+        for way, (origin, target) in enumerate(((near, far), (far, near))):
+            ref = piece(p, section, z, origin)
+            remote(
+                ref, ref, rs.at[way, p, k], rr.at[way, p, k], {"replica": origin}
+            ).wait_recv()
+            if by_near == (way == 0):
+                copy = remote(ref, ref, ds.at[p, k], dr.at[p, k], {"replica": target})
+                copy.start()
+                sent.append(copy)
+            to_core(p, k, 1 + way, origin)
+
+    def third_hop(p, k):
+        z = lax.rem(shard + nz - k, nz)
+        ref = piece(p, section, z, across)
+        by_near = (p + (k if p in (0, 3) else 0)) % 2 == 0
+        origin = far if by_near else near
+        remote(ref, ref, ds.at[p, k], dr.at[p, k], {"replica": origin}).wait_recv()
+        to_core(p, k, 3, across)
+
+    for step in range(6):
+        if step < 4:
+            for k in order:
+                first_hop(step, k)
+        if 1 <= step < 5:
+            for k in order:
+                second_hop(step - 1, k)
+        if step >= 2:
+            for k in order:
+                third_hop(step - 2, k)
+    for copy in arrivals:
+        copy.wait_recv()
+    for copy in sent:
+        copy.wait_send()
+    for copy in locals_here:
+        copy.wait()
+
+
+def gather_weights(attn_in, out_proj, mlp_in, mlp_out):
+    nz = lax.axis_size("shard")
+    joined = jnp.concatenate([attn_in, out_proj], axis=1)
+    rows, a_cols = joined.shape
+    m_cols = mlp_in.shape[1]
+    down_rows, d_model = mlp_out.shape
+    m_in = mlp_in.reshape(2, rows // 2, m_cols)
+    o_in = mlp_out.reshape(4, down_rows // 4, d_model)
+    dma = pltpu.SemaphoreType.DMA
+    a_all, m_all, o_all = pl.pallas_call(
+        gather_kernel,
+        out_shape=(
+            jax.ShapeDtypeStruct((2, nz) + joined.shape, jnp.bfloat16),
+            jax.ShapeDtypeStruct((2, nz) + m_in.shape, jnp.bfloat16),
+            jax.ShapeDtypeStruct((2, nz) + o_in.shape, jnp.bfloat16),
+        ),
+        in_specs=[pl.BlockSpec(memory_space=pl.ANY)] * 3,
+        out_specs=(pl.BlockSpec(memory_space=pl.ANY),) * 3,
+        scratch_shapes=[
+            dma((3,)),
+            dma((4, nz)),
+            dma((4, nz)),
+            dma((2, 4, nz)),
+            dma((2, 4, nz)),
+            dma((4, nz)),
+            dma((4, nz)),
+            dma((3,)),
+            dma((3,)),
+            dma((4, 4, nz)),
+            dma((4, 4, nz)),
+        ],
+        compiler_params=pltpu.CompilerParams(collective_id=0, has_side_effects=True),
+    )(joined, m_in, o_in)
+    return (
+        a_all.reshape(2, nz * rows, a_cols),
+        m_all.reshape(2, nz * rows, m_cols),
+        o_all.reshape(2, nz * down_rows, d_model),
+    )
+
+
+def swap_cores(value):
+    return lax.ppermute(value, "section", [(0, 1), (1, 0)])
+
+
+def scatter_shards(value):
+    nz = lax.axis_size("shard")
+    shard = lax.axis_index("shard")
+    total = lax.dynamic_index_in_dim(value, shard, 0, keepdims=False).astype(jnp.float32)
+    for k in range(1, nz):
+        block = lax.dynamic_index_in_dim(value, lax.rem(shard + k, nz), 0, keepdims=False)
+        block = lax.ppermute(block, "shard", [(i, (i + k) % nz) for i in range(nz)])
+        total = total + block.astype(jnp.float32)
+    return brain_float(total)
+
+
+def reduce_group(send, keep):
+    half = brain_float(keep.astype(jnp.float32) + swap_cores(send).astype(jnp.float32))
+    part = lax.psum_scatter(half, "replica", scatter_dimension=0, tiled=True)
+    nz = lax.axis_size("shard")
+    block = scatter_shards(part.reshape(nz, part.shape[0] // nz, part.shape[1]))
+    return lax.all_gather(block, "replica", axis=0, tiled=True)
+
+
+def replica_major(values, inner):
+    nz = lax.axis_size("shard")
+    rows = values.shape[0]
+    width = values.shape[1] // (inner * 4 * nz)
+    return (
+        values.reshape(rows, nz, inner, 4, width)
+        .transpose(0, 2, 3, 1, 4)
+        .reshape(rows, values.shape[1])
+    )
+
+
+def picked(section_id, first, second):
+    return jnp.where(section_id == 0, second, first), jnp.where(section_id == 0, first, second)
+
+
+def mlp_weight_grads(section_id, normed_two, gate_up_low, activated, cotangent):
+    nz = lax.axis_size("shard")
+    normed_two = replica_major(normed_two, 1)
+    send, keep = picked(section_id, gate_up_low[:, :FF], gate_up_low[:, FF:])
+    grad_m = reduce_group(
+        brain_float(matmul_left(normed_two, send)), brain_float(matmul_left(normed_two, keep))
+    )
+    send, keep = picked(section_id, cotangent[:, : D // 2], cotangent[:, D // 2 :])
+
+    def down(half):
+        grad = brain_float(matmul_left(activated, half))
+        rows = grad.shape[0]
+        return (
+            grad.reshape(nz, 4, rows // (4 * nz), D // 2).transpose(1, 0, 2, 3).reshape(rows, D // 2)
+        )
+
+    return grad_m, reduce_group(down(send), down(keep))
+
+
+def attention_weight_grads(section_id, normed, project_low, attended_low, branch_low):
+    normed = replica_major(normed, 2)
+    attended_low = replica_major(attended_low, 2)
+    normed_send, normed_keep = picked(section_id, normed[:, : D // 2], normed[:, D // 2 :])
+    attended_send, attended_keep = picked(
+        section_id, attended_low[:, : D // 2], attended_low[:, D // 2 :]
+    )
+
+    def grads(first, second):
+        return brain_float(
+            jnp.concatenate(
+                [matmul_left(first, project_low), matmul_left(second, branch_low)], axis=1
+            )
+        )
+
+    return reduce_group(grads(normed_send, attended_send), grads(normed_keep, attended_keep))
+
+
 def local(edges, positions, attn_in, out_proj, mlp_in, mlp_out, gains, bias):
     section_id = lax.axis_index("section")
     shard_id = lax.axis_index("shard")
-    shard_count = lax.axis_size("shard")
-    micro_count = edges.shape[1]
     count_of_rows = edges.shape[3]
-    local_data = edges[0, :, 0]
-    all_pos = positions[:, 0]
+    first = section_id == 0
+    own = edges[0, :, 0]
+    incoming = swap_cores(jnp.where(first, own[1], own[0]))
+    block_in = jnp.where(first, own[0], incoming)
+    cotangent = jnp.where(first, incoming, own[1])
+    token_pos = lax.dynamic_index_in_dim(positions[:, 0], section_id, 0, keepdims=False)
     row_index = shard_id * count_of_rows + jnp.arange(count_of_rows, dtype=jnp.int32)
-    gathered = (
-        lax.all_gather(attn_in, "shard", axis=1, tiled=True),
-        lax.all_gather(out_proj, "shard", axis=1, tiled=True),
-        lax.all_gather(mlp_in, "shard", axis=1, tiled=True),
-        lax.all_gather(mlp_out, "shard", axis=1, tiled=True),
-        lax.all_gather(gains, "shard", axis=1, tiled=True),
-        lax.all_gather(bias, "shard", axis=1, tiled=True),
-    )
-    forward_weights = tuple((gathered_one[0] for gathered_one in gathered))
-    received = jnp.zeros((count_of_rows, D), jnp.bfloat16)
+    gain_rows = gains.shape[1]
+    vectors = lax.all_gather(
+        jnp.concatenate([gains[0], bias[0]]), ("section", "shard"), axis=0, tiled=False
+    ).reshape(2, -1, gain_rows + bias.shape[1])
+    gain_full = vectors[:, :, :gain_rows].reshape(2, -1)
+    bias_full = vectors[:, :, gain_rows:].reshape(2, -1)
+    a_all, m_all, o_all = gather_weights(attn_in[0], out_proj[0], mlp_in[0], mlp_out[0])
+    weights = [
+        (a_all[l][:, :QKV], a_all[l][:, QKV:], m_all[l], o_all[l], gain_full[l], bias_full[l])
+        for l in range(2)
+    ]
+    saved_all = []
     outputs = []
-    saved_all = []
-    for moment in range(micro_count + 1):
-        micro_id = moment - section_id
-        active = (micro_id >= 0) & (micro_id < micro_count)
-        chosen = jnp.clip(micro_id, 0, micro_count - 1)
-        own_block = lax.dynamic_index_in_dim(local_data, chosen, 0, keepdims=False)
-        token_pos = lax.dynamic_index_in_dim(all_pos, chosen, 0, keepdims=False)
-        block_in = jnp.where(section_id == 0, own_block, received)
-        first_part = when_active(active, attention_inputs, (block_in, token_pos, forward_weights))
-        keys_all, value_rows_every = (
-            lax.all_gather(first_part[3], "shard", axis=0, tiled=True),
-            lax.all_gather(first_part[4], "shard", axis=0, tiled=True),
-        )
-        second_part = when_active(
-            active,
-            finish_forward,
-            (
-                block_in,
-                token_pos,
-                row_index,
-                first_part,
-                keys_all,
-                value_rows_every,
-                forward_weights,
-            ),
-        )
-        outputs.append(second_part[0])
-        saved_all.append((block_in, token_pos, first_part, keys_all, value_rows_every, second_part))
-        if moment < micro_count:
-            received = shifted(second_part[0], "section", 1)
-    received_grad = jnp.zeros((count_of_rows, D), jnp.bfloat16)
-    grads_out = []
-    records = []
-    gain_sum = jnp.zeros((2 * D,), jnp.float32)
-    bias_sum = jnp.zeros((QKV,), jnp.float32)
-    for moment in range(micro_count + 1):
-        micro_id = moment - (1 - section_id)
-        active = (micro_id >= 0) & (micro_id < micro_count)
-        chosen = jnp.clip(micro_id, 0, micro_count - 1)
-        own_block = lax.dynamic_index_in_dim(local_data, chosen, 0, keepdims=False)
-        cotangent = jnp.where(section_id == 1, own_block, received_grad)
-        earlier = saved_all[max(moment - 1, 0)]
-        later_one = saved_all[min(moment + 1, micro_count)]
-        saved_now = jax.tree.map(
-            lambda low_side, high_side: jnp.where(section_id == 0, low_side, high_side),
-            earlier,
-            later_one,
-        )
-        back_part = when_active(
-            active, backward_branches, (cotangent, saved_now, row_index, forward_weights)
-        )
-        key_gradients, value_grads = (
-            lax.psum_scatter(
-                back_part[1].astype(jnp.bfloat16), "shard", scatter_dimension=0, tiled=True
-            ).astype(jnp.float32),
-            lax.psum_scatter(
-                back_part[2].astype(jnp.bfloat16), "shard", scatter_dimension=0, tiled=True
-            ).astype(jnp.float32),
-        )
-        final_part = when_active(
-            active,
-            backward_inputs,
-            (back_part, key_gradients, value_grads, saved_now, forward_weights),
-        )
-        grads_out.append(final_part[0])
-        first_saved = saved_now[2]
-        second_saved = saved_now[5]
-        records.append(
-            (
-                first_saved[0],
-                final_part[1],
-                second_saved[2],
-                back_part[4],
-                second_saved[5],
-                back_part[5],
-                second_saved[7],
-                cotangent,
-            )
-        )
-        gain_sum = gain_sum + final_part[2]
-        bias_sum = bias_sum + final_part[3]
-        if moment < micro_count:
-            received_grad = shifted(brain_float(final_part[0]), "section", -1)
-
-    def by_micro(series, zero_offset, one_offset):
-        return [
-            jax.tree.map(
-                lambda zero_side, one_side: jnp.where(section_id == 0, zero_side, one_side),
-                series[micro_index + zero_offset],
-                series[micro_index + one_offset],
-            )
-            for micro_index in range(micro_count)
-        ]
-
-    layer_outputs = jnp.stack(by_micro(outputs, 0, 1), axis=0)[None, :, None]
-    input_grads = jnp.stack(by_micro(grads_out, 1, 0), axis=0)[None, :, None]
-    chosen_records = by_micro(records, 1, 0)
-    joined = tuple(
-        (
-            jnp.concatenate([record_one[field_id] for record_one in chosen_records], axis=0)
-            for field_id in range(8)
-        )
-    )
-    grad_attn = matmul_left(joined[0], joined[1])
-    grad_out = matmul_left(joined[2], joined[3])
-    grad_mlp = matmul_left(joined[4], joined[5])
-    grad_down = matmul_left(joined[6], joined[7])
+    key_width = KEY_VALUE_HEADS * HEAD_SIZE
+    for layer in range(2):
+        first_part = attention_inputs(block_in, token_pos, weights[layer])
+        both = lax.all_gather(
+            jnp.concatenate([first_part[3], first_part[4]], axis=1), "shard", axis=0, tiled=True
+        )
+        keys_all, values_all = both[:, :key_width], both[:, key_width:]
+        second_part = finish_forward(
+            block_in, token_pos, row_index, first_part, keys_all, values_all, weights[layer]
+        )
+        saved_all.append((block_in, token_pos, first_part, keys_all, values_all, second_part))
+        block_in = second_part[0]
+        outputs.append(block_in)
+    grads_out = [None, None]
+    reduced = [None, None]
+    small = [None, None]
+    for layer in (1, 0):
+        saved_now = saved_all[layer]
+        first_saved, second_saved = saved_now[2], saved_now[5]
+        mlp_part = backward_mlp(cotangent, saved_now, weights[layer])
+        grad_m, grad_o = mlp_weight_grads(
+            section_id, second_saved[5], mlp_part[0], second_saved[7], cotangent
+        )
+        back_part = backward_branches(cotangent, mlp_part, saved_now, row_index, weights[layer])
+        both = lax.psum_scatter(
+            brain_float(jnp.concatenate([back_part[1], back_part[2]], axis=1)),
+            "shard",
+            scatter_dimension=0,
+            tiled=True,
+        ).astype(jnp.float32)
+        final_part = backward_inputs(
+            back_part, both[:, :key_width], both[:, key_width:], saved_now, weights[layer]
+        )
+        grad_a = attention_weight_grads(
+            section_id, first_saved[0], final_part[1], second_saved[2], back_part[4]
+        )
+        reduced[layer] = (grad_a, grad_m, grad_o)
+        small[layer] = jnp.concatenate([final_part[2], final_part[3]])
+        grads_out[layer] = final_part[0]
+        cotangent = brain_float(final_part[0])
+
+    def by_micro(pair):
+        moved = swap_cores(jnp.where(first, pair[1], pair[0]))
+        return jnp.stack(
+            [jnp.where(first, pair[0], moved), jnp.where(first, moved, pair[1])], axis=0
+        )[None, :, None]
+
+    layer_outputs = by_micro(outputs)
+    input_grads = by_micro(grads_out)
+    halves = []
+    for zero, one in zip(reduced[0], reduced[1]):
+        moved = swap_cores(jnp.where(first, one, zero)).astype(jnp.float32)
+        kept = jnp.where(first, zero, one).astype(jnp.float32)
+        halves.append((jnp.where(first, kept, moved), jnp.where(first, moved, kept)))
+    grad_a = jnp.concatenate(halves[0], axis=0)
+    grad_m = jnp.concatenate(halves[1], axis=1)
+    grad_o = jnp.concatenate(halves[2], axis=1)
+    sums = lax.psum(jnp.stack(small), ("section", "shard", "replica"))
+    mine = lax.dynamic_index_in_dim(sums, section_id, 0, keepdims=False)
+
+    def block(values):
+        count = values.shape[0] // lax.axis_size("shard")
+        return lax.dynamic_slice_in_dim(values, shard_id * count, count, 0)[None]
+
     query_key = (QUERY_HEADS + KEY_VALUE_HEADS) * HEAD_SIZE
-    value_width = KEY_VALUE_HEADS * HEAD_SIZE
-    arranged = jnp.concatenate(
-        [
-            bias_sum[:query_key].reshape(shard_count, query_key // shard_count),
-            bias_sum[query_key:].reshape(shard_count, value_width // shard_count),
-        ],
-        axis=1,
-    ).reshape(QKV)
-    summed = (
-        lax.psum_scatter(
-            grad_attn.astype(jnp.bfloat16), "shard", scatter_dimension=0, tiled=True
-        ).astype(jnp.float32),
-        lax.psum_scatter(
-            grad_out.astype(jnp.bfloat16), "shard", scatter_dimension=0, tiled=True
-        ).astype(jnp.float32),
-        lax.psum_scatter(
-            grad_mlp.astype(jnp.bfloat16), "shard", scatter_dimension=0, tiled=True
-        ).astype(jnp.float32),
-        lax.psum_scatter(
-            grad_down.astype(jnp.bfloat16), "shard", scatter_dimension=0, tiled=True
-        ).astype(jnp.float32),
-        lax.psum_scatter(
-            gain_sum.astype(jnp.bfloat16), "shard", scatter_dimension=0, tiled=True
-        ).astype(jnp.float32),
-        lax.psum_scatter(
-            arranged.astype(jnp.bfloat16), "shard", scatter_dimension=0, tiled=True
-        ).astype(jnp.float32),
-    )
-    totals = (
-        lax.psum(summed[0].astype(jnp.bfloat16), "replica").astype(jnp.float32),
-        lax.psum(summed[1].astype(jnp.bfloat16), "replica").astype(jnp.float32),
-        lax.psum(summed[2].astype(jnp.bfloat16), "replica").astype(jnp.float32),
-        lax.psum(summed[3].astype(jnp.bfloat16), "replica").astype(jnp.float32),
-        lax.psum(summed[4].astype(jnp.bfloat16), "replica").astype(jnp.float32),
-        lax.psum(summed[5].astype(jnp.bfloat16), "replica").astype(jnp.float32),
-    )
-    bias_block = totals[5]
-    query_key_part = bias_block[: query_key // shard_count]
-    value_part = bias_block[query_key // shard_count :]
     return (
         layer_outputs,
         input_grads,
-        totals[0][None],
-        totals[1][None],
-        totals[2][None],
-        totals[3][None],
-        totals[4][None],
-        query_key_part[None],
-        value_part[None],
+        grad_a[None, :, :QKV],
+        grad_a[None, :, QKV:],
+        grad_m[None],
+        grad_o[None],
+        block(mine[: 2 * D]),
+        block(mine[2 * D : 2 * D + query_key]),
+        block(mine[2 * D + query_key :]),
     )
 
 

time: 1980 us -> 1240 us (0.63)
  waiting for transfers between devices: 1260 us -> 244 us
  Pallas kernels: 0 us -> 258 us
  local copies, waits for them, and re-layouts: 58.7 us -> 196 us
  starting transfers between devices: 99.2 us -> 38.1 us
  other arithmetic: 158 us -> 108 us
  blocking collectives: 124 us -> 144 us
    reduce_scatter x10 -> x8, waiting for transfers between devices: 619 us -> 54.8 us  [the longest x6 54.8 us: reduce_group(): part = lax.psum_scatter(half, 'replica', scatter_dimension=0, tiled=True)]
    all_gather x4, waiting for transfers between devices: 488 us -> 65.7 us  [reduce_group(): return lax.all_gather(block, 'replica', axis=0, tiled=True)]
    pallas_call x0 -> x1, Pallas kernels: none -> 258 us  [gather_weights(): pl.pallas_call(gather_kernel, out_shape=(jax.ShapeDtypeStruct((2, nz) + j...]
    psum x1 -> x0, waiting for transfers between devices: 135 us -> none  [local(): lax.psum(summed[0].astype(jnp.bfloat16), 'replica').astype(jnp.float32)]
    ppermute x4 -> x30, waiting for transfers between devices: 12.7 us -> 124 us  [the longest x18 108 us: scatter_shards(): block = lax.ppermute(block, 'shard', [(i, (i + k) % nz) for i in range(nz)])]
    ppermute x4 -> x30, starting transfers between devices: 98.4 us -> 37.1 us  [the longest x18 32.2 us: scatter_shards(): block = lax.ppermute(block, 'shard', [(i, (i + k) % nz) for i in range(nz)])]
    slice x4 -> x10, local copies, waits for them, and re-layouts: 0.66 us -> 45.7 us  [the longest x1 23.1 us: local(): m_all[l]]
    select_n x23 -> x9, other arithmetic: 54.5 us -> 12.9 us  [the longest x3 4.73 us: local(): moved = swap_cores(jnp.where(first, one, zero)).astype(jnp.float32)]
  transfers between devices with their start and end apart: 19 -> 42, of which waited for: 17 -> 15; matrix products, arithmetic and copies ran while one was open for 4% -> 30% of each run, Pallas kernels for 0% -> 21%
where the time goes in v1:
time: 1240 us; the launch traced here: 1230 us
  Pallas kernels  258 us (21%)
  waiting for transfers between devices  244 us (20%)
  matrix products  223 us (18%)
  local copies, waits for them, and re-layouts  196 us (16%)
  blocking collectives  144 us (12%)
  other arithmetic  108 us (9%)
  starting transfers between devices  38.1 us (3%)
  between operations  17.6 us (1%)
    pallas_call x1, Pallas kernels, gather_weights(): pl.pallas_call(gather_kernel, out_shape=(jax.ShapeDtypeStruct((2, nz) + j...  258 us
    ppermute x18, waiting for transfers between devices, scatter_shards(): block = lax.ppermute(block, 'shard', [(i, (i + k) % nz) for i in range(nz)])  108 us
    dot_general x8, matrix products, matmul_right(): lax.dot_general(first_mat, second_mat, (((1,), (1,)), ((), ())), preferre...  73 us
    all_gather x4, waiting for transfers between devices, reduce_group(): return lax.all_gather(block, 'replica', axis=0, tiled=True)  65.7 us
    convert_element_type x20, other arithmetic, brain_float(): return values.astype(jnp.bfloat16)  59.8 us
    reduce_scatter x6, waiting for transfers between devices, reduce_group(): part = lax.psum_scatter(half, 'replica', scatter_dimension=0, tiled=True)  54.8 us
    dot_general x16, matrix products, matmul_left(): lax.dot_general(first_mat, second_mat, (((0,), (0,)), ((), ())), preferre...  51.3 us
    psum x1, blocking collectives, local(): sums = lax.psum(jnp.stack(small), ('section', 'shard', 'replica'))  50.3 us
  transfers between devices with their start and end apart: 42, of which 15 were waited for; matrix products, arithmetic and copies ran while one was open for 30% of the time, Pallas kernels for 21%

profile of v1, /device:TPU:0, one launch (start us, length us, event | category | flops | bytes accessed | tf_op | source)
XLA Modules:
  0.0 1229.1 jit_solution(11313301912146900224)
XLA Ops:
  12.5 30.7 %all-reduce = bf16[5888]{0:T(1024)(128)(2,1)S(1)} all-reduce(bf16[5888]{0:T(1024)(128)(2,1)S(1)} %dynamic-update-slice), channel_id=2, replica_groups=mesh['section'=2,'shard'=4,'replica'=4] {'section','shard'}, use_global_device_ids=true, to_apply=%add | all-reduce | flops 5888 | bytes 23552
  45.6 257.5 %shard_map.151 = (bf16[2,4,224,2048]{3,2,1,0:T(8,128)(2,1)}, bf16[2,4,2,112,9728]{4,3,2,1,0:T(8,128)(2,1)}, bf16[2,4,4,304,896]{4,3,2,1,0:T(8,128)(2,1)}) custom-call(bf16[224,2048]{1,0:T(8,128)(2,1)} %pad_maximum_fusion.2.a_in, bf16[2,112,9728]{2,1,0:T(8,128)(2,1)} %bitcast.485, bf16[4,304,896]{2,1,0:T(8,128)(2,1)} %bitcast.506), custom_call_target="tpu_custom_call" | custom-call | tf_op jit(solution)/shard_map/pallas_call | solution.py:444
  310.5 23.1 %fusion.233 = (bf16[1,4,2,112,9728]{4,3,2,1,0:T(8,128)(2,1)}, bf16[1,4,2,112,9728]{4,3,2,1,0:T(8,128)(2,1)}) fusion(bf16[2,4,2,112,9728]{4,3,2,1,0:T(8,128)(2,1)} %get-tuple-element.13), kind=kLoop, calls=%fused_computation.417 | loop fusion | bytes 69730304 | tf_op jit(solution)/shard_map/slice | solution.py:569
  333.7 12.0 fusion.234
  350.8 21.4 %all_gather.32 = bf16[1024,256]{1,0:T(8,128)(2,1)S(1)} all-gather(bf16[256,256]{1,0:T(8,128)(2,1)S(1)} %pad_maximum_fusion.14), channel_id=1, replica_groups=mesh['section'=2,'shard'=4,'replica'=4] {'shard'}, dimensions={0}, use_global_device_ids=true | all-gather | bytes 655360 | tf_op jit(solution)/shard_map/all_gather | solution.py:577
  403.1 16.5 %all_gather.33 = bf16[1024,256]{1,0:T(8,128)(2,1)S(1)} all-gather(bf16[256,256]{1,0:T(8,128)(2,1)S(1)} %pad_maximum_fusion.15), channel_id=1, replica_groups=mesh['section'=2,'shard'=4,'replica'=4] {'shard'}, dimensions={0}, use_global_device_ids=true | all-gather | bytes 655360 | tf_op jit(solution)/shard_map/all_gather | solution.py:577
  445.8 11.9 multiply_convert_fusion.3
  457.6 19.9 %multiply_reduce_fusion = (f32[896]{0:T(1024)}, f32[256]{0:T(256)S(1)}, f32[256,896]{1,0:T(8,128)}) fusion(f32[256,896]{1,0:T(8,128)} %copy-done.57, f32[256]{0:T(256)S(1)} %add_rsqrt_fusion, f32[896]{0:T(1024)S(1)} %reshape.500, bf16[896,9728]{1,0:T(8,128)(2,1)} %bitcast.449, bf16[256,4864]{1,0:T(8,128)(2,1)} %get-tuple-element.70, ...), kind=kOutput, calls=%fused_computation.226 | convolution fusion | flops 4474076160 | bytes 24257536 | tf_op jit(solution)/shard_map/dot_general | solution.py:37
  576.2 11.3 multiply_convert_fusion.1
  587.6 19.7 %multiply_reduce_fusion.1 = (f32[896]{0:T(1024)}, f32[256]{0:T(256)}, f32[256,896]{1,0:T(8,128)}) fusion(f32[256,896]{1,0:T(8,128)S(1)} %copy-done.60, f32[256]{0:T(256)S(1)} %copy-done.117, f32[896]{0:T(1024)S(1)} %copy-done.107, bf16[896,9728]{1,0:T(8,128)(2,1)} %bitcast.445, bf16[256,4864]{1,0:T(8,128)(2,1)} %get-tuple-element.68, ...), kind=kOutput, calls=%fused_computation.227 | convolution fusion | flops 4474076160 | bytes 24257536 | tf_op jit(solution)/shard_map/dot_general | solution.py:37
  762.9 13.6 %collective-permute-done.12 = bf16[896,4864]{1,0:T(8,128)(2,1)S(1)} collective-permute-done((bf16[896,4864]{1,0:T(8,128)(2,1)S(1)}, bf16[896,4864]{1,0:T(8,128)(2,1)S(1)}, u32[]{:S(2)}, u32[]{:S(2)}) %collective-permute-start.12) | collective-permute-done | bytes 8716320 | tf_op jit(solution)/shard_map/ppermute | solution.py:476
  834.3 12.3 %collective-permute-done.27 = bf16[304,448]{1,0:T(8,128)(2,1)} collective-permute-done((bf16[304,448]{1,0:T(8,128)(2,1)}, bf16[304,448]{1,0:T(8,128)(2,1)}, u32[]{:S(2)}, u32[]{:S(2)}) %collective-permute-start.27) | collective-permute-done | bytes 272416 | tf_op jit(solution)/shard_map/ppermute | solution.py:485
  865.8 12.2 collective-permute-done.23
  880.1 12.2 reduce-scatter.19.cloned.1.call-done
  911.0 22.1 %collective-permute-done.18 = bf16[56,4864]{1,0:T(8,128)(2,1)S(1)} collective-permute-done((bf16[56,4864]{1,0:T(8,128)(2,1)S(1)}, bf16[56,4864]{1,0:T(8,128)(2,1)S(1)}, u32[]{:S(2)}, u32[]{:S(2)}) %collective-permute-start.18) | collective-permute-done | bytes 544800 | tf_op jit(solution)/shard_map/ppermute | solution.py:485
  941.8 42.6 %reduce-scatter.17.cloned.1.call-done = bf16[224,4864]{1,0:T(8,128)(2,1)} async-done(((bf16[896,4864]{1,0:T(8,128)(2,1)}), bf16[224,4864]{1,0:T(8,128)(2,1)}) %reduce-scatter.17.cloned.1.call-update) | async-done | bytes 2179088 | tf_op jit(solution)/shard_map/reduce_scatter | solution.py:492
  992.5 10.6 collective-permute-done.13
  1003.2 22.1 %collective-permute-done.14 = bf16[56,4864]{1,0:T(8,128)(2,1)S(1)} collective-permute-done((bf16[56,4864]{1,0:T(8,128)(2,1)S(1)}, bf16[56,4864]{1,0:T(8,128)(2,1)S(1)}, u32[]{:S(2)}, u32[]{:S(2)}) %collective-permute-start.14) | collective-permute-done | bytes 544800 | tf_op jit(solution)/shard_map/ppermute | solution.py:485
  1027.5 50.3 %psum.7 = f32[2,2944]{1,0:T(2,128)S(1)} all-reduce(f32[2,2944]{1,0:T(2,128)S(1)} %pad_maximum_fusion.20), channel_id=1, replica_groups=mesh['section'=2,'shard'=4,'replica'=4] {'section','shard','replica'}, use_global_device_ids=true, to_apply=%region_34.35 | all-reduce | flops 5888 | bytes 47104 | tf_op jit(solution)/shard_map/psum | solution.py:631
  1093.5 10.3 collective-permute-done.9
  1103.8 14.6 %all-gather.2 = bf16[4,28,2048]{2,1,0:T(8,128)(2,1)S(1)} all-gather(bf16[1,28,2048]{2,1,0:T(8,128)(2,1)S(1)} %fusion.209), channel_id=1, replica_groups=mesh['section'=2,'shard'=4,'replica'=4] {'replica'}, dimensions={0}, use_global_device_ids=true | all-gather | bytes 573440 | tf_op jit(solution)/shard_map/all_gather | solution.py:495
  1118.5 10.4 all-gather.1
  1133.5 27.4 %all-gather.10.cloned.1.call-done = bf16[224,4864]{1,0:T(8,128)(2,1)} async-done(((bf16[56,4864]{1,0:T(8,128)(2,1)}), bf16[224,4864]{1,0:T(8,128)(2,1)}) %all-gather.10.cloned.1.call-update) | async-done | bytes 2179088 | tf_op jit(solution)/shard_map/all_gather | solution.py:495
  1160.9 38.3 %all-gather.8.cloned.1.call-done = bf16[224,4864]{1,0:T(8,128)(2,1)} async-done(((bf16[56,4864]{1,0:T(8,128)(2,1)}), bf16[224,4864]{1,0:T(8,128)(2,1)}) %all-gather.8.cloned.1.call-update) | async-done | bytes 2179088 | tf_op jit(solution)/shard_map/all_gather | solution.py:495
  (620 shorter events, 488.3 us)
Async XLA Ops:
  7.2 563.5 %reduce-scatter.9.cloned.1.call-start = ((), (), s32[]{:S(2)}) async-start(), calls=%async_computation.8 | async-start | bytes 655360 | tf_op jit(solution)/shard_map/reduce_scatter | solution.py:598
  8.5 338.8 %collective-permute-start = (bf16[256,896]{1,0:T(8,128)(2,1)S(1)}, bf16[256,896]{1,0:T(8,128)(2,1)S(1)}, u32[]{:S(2)}, u32[]{:S(2)}) collective-permute-start(bf16[256,896]{1,0:T(8,128)(2,1)S(1)} %bitcast_select_fusion.5), channel_id=1, source_target_pairs={{0,16},{16,0},{1,17},{17,1},{2,18},{18,2},{3,19},{19,3},{4,20},{20... | collective-permute-start | bytes 1376264 | tf_op jit(solution)/shard_map/ppermute | solution.py:476
  526.7 283.7 %reduce-scatter.11.cloned.1.call-start = ((), (), s32[]{:S(2)}) async-start(), calls=%async_computation.9 | async-start | bytes 655360 | tf_op jit(solution)/shard_map/reduce_scatter | solution.py:598
  569.6 77.9 %collective-permute-start.25 = (bf16[4864,448]{0,1:T(8,128)(2,1)}, bf16[4864,448]{0,1:T(8,128)(2,1)}, u32[]{:S(2)}, u32[]{:S(2)}) collective-permute-start(bf16[4864,448]{0,1:T(8,128)(2,1)} %copy.290), channel_id=1, source_target_pairs={{0,16},{16,0},{1,17},{17,1},{2,18},{18,2},{3,19},{19,3},{4,20},{20... | collective-permute-start | bytes 13074440 | tf_op jit(solution)/shard_map/ppermute | solution.py:476
  647.4 172.3 %reduce-scatter.23.cloned.1.call-start = ((), (), s32[]{:S(2)}) async-start(), calls=%async_computation.18 | async-start | bytes 6225920 | tf_op jit(solution)/shard_map/reduce_scatter | solution.py:492
  664.1 184.7 %reduce-scatter.21.cloned.1.call-start = ((), (), s32[]{:S(2)}) async-start(), calls=%async_computation.16 | async-start | bytes 6225920 | tf_op jit(solution)/shard_map/reduce_scatter | solution.py:492
  690.4 35.9 %collective-permute-start.21 = (bf16[4864,448]{0,1:T(8,128)(2,1)}, bf16[4864,448]{0,1:T(8,128)(2,1)}, u32[]{:S(2)}, u32[]{:S(2)}) collective-permute-start(bf16[4864,448]{0,1:T(8,128)(2,1)} %copy.284), channel_id=1, source_target_pairs={{0,16},{16,0},{1,17},{17,1},{2,18},{18,2},{3,19},{19,3},{4,20},{20... | collective-permute-start | bytes 13074440 | tf_op jit(solution)/shard_map/ppermute | solution.py:476
  701.8 41.1 %collective-permute-start.16 = (bf16[896,4864]{1,0:T(8,128)(2,1)}, bf16[896,4864]{1,0:T(8,128)(2,1)}, u32[]{:S(2)}, u32[]{:S(2)}) collective-permute-start(bf16[896,4864]{1,0:T(8,128)(2,1)} %convolution_convert_fusion), channel_id=1, source_target_pairs={{0,16},{16,0},{1,17},{17,1},{2,18},{18,2},{3,19},{19,3},{4,20},{20... | collective-permute-start | bytes 26148872 | tf_op jit(solution)/shard_map/ppermute | solution.py:476
  742.8 149.5 %reduce-scatter.19.cloned.1.call-start = ((), (), s32[]{:S(2)}) async-start(), calls=%async_computation.14 | async-start | bytes 10895360 | tf_op jit(solution)/shard_map/reduce_scatter | solution.py:492
  754.7 229.7 %reduce-scatter.17.cloned.1.call-start = ((), (), s32[]{:S(2)}) async-start(), calls=%async_computation.12 | async-start | bytes 10895360 | tf_op jit(solution)/shard_map/reduce_scatter | solution.py:492
  781.5 301.0 %reduce-scatter.15.cloned.1.call-start = ((), (), s32[]{:S(2)}) async-start(), calls=%async_computation.11 | async-start | bytes 2293760 | tf_op jit(solution)/shard_map/reduce_scatter | solution.py:492
  809.9 277.2 %reduce-scatter.13.cloned.1.call-start = ((), (), s32[]{:S(2)}) async-start(), calls=%async_computation.10 | async-start | bytes 2293760 | tf_op jit(solution)/shard_map/reduce_scatter | solution.py:492
  819.6 310.3 %all-gather.14.cloned.1.call-start = ((), (), s32[]{:S(2)}) async-start(), calls=%async_computation.19 | async-start | bytes 1556480 | tf_op jit(solution)/shard_map/all_gather | solution.py:495
  848.8 281.2 %all-gather.12.cloned.1.call-start = ((), (), s32[]{:S(2)}) async-start(), calls=%async_computation.17 | async-start | bytes 1556480 | tf_op jit(solution)/shard_map/all_gather | solution.py:495
  880.1 280.8 %all-gather.10.cloned.1.call-start = ((), (), s32[]{:S(2)}) async-start(), calls=%async_computation.15 | async-start | bytes 2723840 | tf_op jit(solution)/shard_map/all_gather | solution.py:495
  895.3 37.8 %collective-permute-start.18 = (bf16[56,4864]{1,0:T(8,128)(2,1)S(1)}, bf16[56,4864]{1,0:T(8,128)(2,1)S(1)}, u32[]{:S(2)}, u32[]{:S(2)}) collective-permute-start(bf16[56,4864]{1,0:T(8,128)(2,1)S(1)} %get-tuple-element.83), channel_id=1, source_target_pairs={{0,8},{4,12},{8,0},{12,4},{1,9},{5,13},{9,1},{13,5},{2,10},{6,14},... | collective-permute-start | bytes 1634312 | tf_op jit(solution)/shard_map/ppermute | solution.py:485
  897.7 35.4 %collective-permute-start.19 = (bf16[56,4864]{1,0:T(8,128)(2,1)S(1)}, bf16[56,4864]{1,0:T(8,128)(2,1)S(1)}, u32[]{:S(2)}, u32[]{:S(2)}) collective-permute-start(bf16[56,4864]{1,0:T(8,128)(2,1)S(1)} %get-tuple-element.82), channel_id=1, source_target_pairs={{0,12},{4,0},{8,4},{12,8},{1,13},{5,1},{9,5},{13,9},{2,14},{6,2},{... | collective-permute-start | bytes 1634312 | tf_op jit(solution)/shard_map/ppermute | solution.py:485
  935.3 263.9 %all-gather.8.cloned.1.call-start = ((), (), s32[]{:S(2)}) async-start(), calls=%async_computation.13 | async-start | bytes 2723840 | tf_op jit(solution)/shard_map/all_gather | solution.py:495
  987.4 37.8 %collective-permute-start.14 = (bf16[56,4864]{1,0:T(8,128)(2,1)S(1)}, bf16[56,4864]{1,0:T(8,128)(2,1)S(1)}, u32[]{:S(2)}, u32[]{:S(2)}) collective-permute-start(bf16[56,4864]{1,0:T(8,128)(2,1)S(1)} %get-tuple-element.80), channel_id=1, source_target_pairs={{0,8},{4,12},{8,0},{12,4},{1,9},{5,13},{9,1},{13,5},{2,10},{6,14},... | collective-permute-start | bytes 1634312 | tf_op jit(solution)/shard_map/ppermute | solution.py:485
  989.9 35.4 %collective-permute-start.15 = (bf16[56,4864]{1,0:T(8,128)(2,1)S(1)}, bf16[56,4864]{1,0:T(8,128)(2,1)S(1)}, u32[]{:S(2)}, u32[]{:S(2)}) collective-permute-start(bf16[56,4864]{1,0:T(8,128)(2,1)S(1)} %get-tuple-element.79), channel_id=1, source_target_pairs={{0,12},{4,0},{8,4},{12,8},{1,13},{5,1},{9,5},{13,9},{2,14},{6,2},{... | collective-permute-start | bytes 1634312 | tf_op jit(solution)/shard_map/ppermute | solution.py:485
  992.5 87.2 %collective-permute-start.2 = (f32[256,896]{1,0:T(8,128)}, f32[256,896]{1,0:T(8,128)}, u32[]{:S(2)}, u32[]{:S(2)}) collective-permute-start(f32[256,896]{1,0:T(8,128)} %broadcast_select_fusion.5), channel_id=1, source_target_pairs={{0,16},{16,0},{1,17},{17,1},{2,18},{18,2},{3,19},{19,3},{4,20},{20... | collective-permute-start | bytes 2752520 | tf_op jit(solution)/shard_map/ppermute | solution.py:476
  1088.3 30.2 %collective-permute-start.4 = (bf16[28,2048]{1,0:T(8,128)(2,1)S(1)}, bf16[28,2048]{1,0:T(8,128)(2,1)S(1)}, u32[]{:S(2)}, u32[]{:S(2)}) collective-permute-start(bf16[28,2048]{1,0:T(8,128)(2,1)S(1)} %get-tuple-element.107), channel_id=1, source_target_pairs={{0,4},{4,8},{8,12},{12,0},{1,5},{5,9},{9,13},{13,1},{2,6},{6,10},{... | collective-permute-start | bytes 344072 | tf_op jit(solution)/shard_map/ppermute | solution.py:485
  1129.9 73.9 %collective-permute-start.11 = (bf16[112,2048]{1,0:T(8,128)(2,1)}, bf16[112,2048]{1,0:T(8,128)(2,1)}, u32[]{:S(2)}, u32[]{:S(2)}) collective-permute-start(bf16[112,2048]{1,0:T(8,128)(2,1)} %reshape.527), channel_id=1, source_target_pairs={{0,16},{16,0},{1,17},{17,1},{2,18},{18,2},{3,19},{19,3},{4,20},{20... | collective-permute-start | bytes 1376264 | tf_op jit(solution)/shard_map/ppermute | solution.py:476
  1133.0 74.1 %collective-permute-start.29 = (bf16[1216,448]{0,1:T(8,128)(2,1)}, bf16[1216,448]{0,1:T(8,128)(2,1)}, u32[]{:S(2)}, u32[]{:S(2)}) collective-permute-start(bf16[1216,448]{0,1:T(8,128)(2,1)} %copy.292), channel_id=1, source_target_pairs={{0,16},{16,0},{1,17},{17,1},{2,18},{18,2},{3,19},{19,3},{4,20},{20... | collective-permute-start | bytes 3268616 | tf_op jit(solution)/shard_map/ppermute | solution.py:476
  (163 other events, 2201.9 us)
Sparse Core Ops, SparseCore 0:
  526.8 19.0 reduce-scatter.8
  647.5 19.1 reduce-scatter.10
  669.8 57.4 reduce-scatter.22
  743.0 57.1 reduce-scatter.20
  803.2 89.0 reduce-scatter.18
  895.3 89.0 reduce-scatter.16
  988.0 32.9 reduce-scatter.14
  1024.7 33.2 reduce-scatter.12
  1059.8 28.5 all-gather.13
  1090.0 31.8 all-gather.11
  1124.3 36.5 all-gather.9
  1163.2 35.9 all-gather.7

commit v2 on v1

--- a/solution.py
+++ b/solution.py
@@ -492,7 +492,16 @@
     part = lax.psum_scatter(half, "replica", scatter_dimension=0, tiled=True)
     nz = lax.axis_size("shard")
     block = scatter_shards(part.reshape(nz, part.shape[0] // nz, part.shape[1]))
-    return lax.all_gather(block, "replica", axis=0, tiled=True)
+    replica = lax.axis_index("replica")
+    rows = block.shape[0]
+    whole = jnp.zeros((4 * rows, block.shape[1]), block.dtype)
+    for mask in range(4):
+        part = block
+        if mask > 0:
+            part = lax.ppermute(block, "replica", [(i, i ^ mask) for i in range(4)])
+        place = jnp.bitwise_xor(replica, mask) * rows
+        whole = lax.dynamic_update_slice_in_dim(whole, part, place, 0)
+    return whole
 
 
 def replica_major(values, inner):

time: 1240 us -> 1230 us (level)
  waiting for transfers between devices: 244 us -> 121 us
  local copies, waits for them, and re-layouts: 196 us -> 277 us
  starting transfers between devices: 38.1 us -> 82.3 us
  blocking collectives: 144 us -> 109 us
    all_gather x4 -> x0, waiting for transfers between devices: 65.7 us -> none  [reduce_group(): return lax.all_gather(block, 'replica', axis=0, tiled=True)]
    reduce_scatter x6, waiting for transfers between devices: 54.8 us -> 0.05 us  [reduce_group(): part = lax.psum_scatter(half, 'replica', scatter_dimension=0, tiled=True)]
    dynamic_update_slice x0 -> x22, local copies, waits for them, and re-layouts: none -> 51.4 us  [reduce_group(): whole = lax.dynamic_update_slice_in_dim(whole, part, place, 0)]
    ppermute x18, waiting for transfers between devices: 108 us -> 67.4 us  [scatter_shards(): block = lax.ppermute(block, 'shard', [(i, (i + k) % nz) for i in range(nz)])]
    ppermute x0 -> x18, waiting for transfers between devices: none -> 29.6 us  [reduce_group(): part = lax.ppermute(block, 'replica', [(i, i ^ mask) for i in range(4)])]
    ppermute x0 -> x18, starting transfers between devices: none -> 25.2 us  [reduce_group(): part = lax.ppermute(block, 'replica', [(i, i ^ mask) for i in range(4)])]
    all_gather x2 -> x0, blocking collectives: 25 us -> none  [reduce_group(): return lax.all_gather(block, 'replica', axis=0, tiled=True)]
    ppermute x18, starting transfers between devices: 32.2 us -> 52.3 us  [scatter_shards(): block = lax.ppermute(block, 'shard', [(i, (i + k) % nz) for i in range(nz)])]
  transfers between devices with their start and end apart: 42 -> 56, of which waited for: 15 -> 14; matrix products, arithmetic and copies ran while one was open for 30% -> 32% of each run, Pallas kernels for 21% -> 21%
where the time goes in v2:
time: 1230 us; the launch traced here: 1210 us
  local copies, waits for them, and re-layouts  277 us (23%)
  Pallas kernels  258 us (21%)
  matrix products  226 us (18%)
  waiting for transfers between devices  121 us (10%)
  other arithmetic  117 us (10%)
  blocking collectives  109 us (9%)
  starting transfers between devices  82.3 us (7%)
  between operations  17.7 us (1%)
    pallas_call x1, Pallas kernels, gather_weights(): pl.pallas_call(gather_kernel, out_shape=(jax.ShapeDtypeStruct((2, nz) + j...  258 us
    dot_general x8, matrix products, matmul_right(): lax.dot_general(first_mat, second_mat, (((1,), (1,)), ((), ())), preferre...  73.3 us
    ppermute x18, waiting for transfers between devices, scatter_shards(): block = lax.ppermute(block, 'shard', [(i, (i + k) % nz) for i in range(nz)])  67.4 us
    convert_element_type x20, other arithmetic, brain_float(): return values.astype(jnp.bfloat16)  60.4 us
    dot_general x16, matrix products, matmul_left(): lax.dot_general(first_mat, second_mat, (((0,), (0,)), ((), ())), preferre...  56.3 us
    ppermute x18, starting transfers between devices, scatter_shards(): block = lax.ppermute(block, 'shard', [(i, (i + k) % nz) for i in range(nz)])  52.3 us
    dynamic_update_slice x22, local copies, waits for them, and re-layouts, reduce_group(): whole = lax.dynamic_update_slice_in_dim(whole, part, place, 0)  51.4 us
    psum x1, blocking collectives, local(): sums = lax.psum(jnp.stack(small), ('section', 'shard', 'replica'))  40.3 us
  transfers between devices with their start and end apart: 56, of which 14 were waited for; matrix products, arithmetic and copies ran while one was open for 32% of the time, Pallas kernels for 21%

profile of v2, /device:TPU:0, one launch (start us, length us, event | category | flops | bytes accessed | tf_op | source)
XLA Modules:
  0.0 1208.7 jit_solution(16081251498790206329)
XLA Ops:
  12.5 30.7 %all-reduce = bf16[5888]{0:T(1024)(128)(2,1)S(1)} all-reduce(bf16[5888]{0:T(1024)(128)(2,1)S(1)} %dynamic-update-slice), channel_id=2, replica_groups=mesh['section'=2,'shard'=4,'replica'=4] {'section','shard'}, use_global_device_ids=true, to_apply=%add | all-reduce | flops 5888 | bytes 23552
  45.6 257.5 %shard_map.151 = (bf16[2,4,224,2048]{3,2,1,0:T(8,128)(2,1)}, bf16[2,4,2,112,9728]{4,3,2,1,0:T(8,128)(2,1)}, bf16[2,4,4,304,896]{4,3,2,1,0:T(8,128)(2,1)}) custom-call(bf16[224,2048]{1,0:T(8,128)(2,1)} %pad_maximum_fusion.2.a_in, bf16[2,112,9728]{2,1,0:T(8,128)(2,1)} %bitcast.475, bf16[4,304,896]{2,1,0:T(8,128)(2,1)} %bitcast.496), custom_call_target="tpu_custom_call" | custom-call | tf_op jit(solution)/shard_map/pallas_call | solution.py:444
  310.7 23.1 %fusion.233 = (bf16[1,4,2,112,9728]{4,3,2,1,0:T(8,128)(2,1)}, bf16[1,4,2,112,9728]{4,3,2,1,0:T(8,128)(2,1)}) fusion(bf16[2,4,2,112,9728]{4,3,2,1,0:T(8,128)(2,1)} %get-tuple-element.13), kind=kLoop, calls=%fused_computation.425 | loop fusion | bytes 69730304 | tf_op jit(solution)/shard_map/slice | solution.py:578
  333.8 11.9 fusion.234
  351.4 21.3 %all_gather.14 = bf16[1024,256]{1,0:T(8,128)(2,1)S(1)} all-gather(bf16[256,256]{1,0:T(8,128)(2,1)S(1)} %pad_maximum_fusion.14), channel_id=1, replica_groups=mesh['section'=2,'shard'=4,'replica'=4] {'shard'}, dimensions={0}, use_global_device_ids=true | all-gather | bytes 655360 | tf_op jit(solution)/shard_map/all_gather | solution.py:586
  403.7 16.4 %all_gather.15 = bf16[1024,256]{1,0:T(8,128)(2,1)S(1)} all-gather(bf16[256,256]{1,0:T(8,128)(2,1)S(1)} %pad_maximum_fusion.15), channel_id=1, replica_groups=mesh['section'=2,'shard'=4,'replica'=4] {'shard'}, dimensions={0}, use_global_device_ids=true | all-gather | bytes 655360 | tf_op jit(solution)/shard_map/all_gather | solution.py:586
  446.1 11.8 multiply_convert_fusion.3
  458.0 19.9 %multiply_reduce_fusion = (f32[896]{0:T(1024)}, f32[256]{0:T(256)S(1)}, f32[256,896]{1,0:T(8,128)}) fusion(f32[256,896]{1,0:T(8,128)} %copy-done.60, f32[256]{0:T(256)S(1)} %add_rsqrt_fusion, f32[896]{0:T(1024)S(1)} %copy-done.112, bf16[896,9728]{1,0:T(8,128)(2,1)} %bitcast.439, bf16[256,4864]{1,0:T(8,128)(2,1)} %get-tuple-element.65, ...), kind=kOutput, calls=%fused_computation.226 | convolution fusion | flops 4474076160 | bytes 24257536 | tf_op jit(solution)/shard_map/dot_general | solution.py:37
  552.9 11.4 multiply_convert_fusion.1
  564.3 19.7 %multiply_reduce_fusion.1 = (f32[896]{0:T(1024)}, f32[256]{0:T(256)}, f32[256,896]{1,0:T(8,128)}) fusion(f32[256,896]{1,0:T(8,128)S(1)} %copy-done.63, f32[256]{0:T(256)S(1)} %copy-done.122, f32[896]{0:T(1024)S(1)} %reshape.497, bf16[896,9728]{1,0:T(8,128)(2,1)} %bitcast.435, bf16[256,4864]{1,0:T(8,128)(2,1)} %get-tuple-element.63, ...), kind=kOutput, calls=%fused_computation.227 | convolution fusion | flops 4474076160 | bytes 24257536 | tf_op jit(solution)/shard_map/dot_general | solution.py:37
  691.3 10.3 copy.209
  701.6 9.4 copy.210
  770.3 10.2 copy.199
  808.0 9.9 add_convert_fusion
  825.8 13.6 %collective-permute-done.18 = bf16[896,4864]{1,0:T(8,128)(2,1)S(1)} collective-permute-done((bf16[896,4864]{1,0:T(8,128)(2,1)S(1)}, bf16[896,4864]{1,0:T(8,128)(2,1)S(1)}, u32[]{:S(2)}, u32[]{:S(2)}) %collective-permute-start.18) | collective-permute-done | bytes 8716320 | tf_op jit(solution)/shard_map/ppermute | solution.py:476
  872.5 40.3 %psum.7 = f32[2,2944]{1,0:T(2,128)S(1)} all-reduce(f32[2,2944]{1,0:T(2,128)S(1)} %pad_maximum_fusion.20), channel_id=1, replica_groups=mesh['section'=2,'shard'=4,'replica'=4] {'section','shard','replica'}, use_global_device_ids=true, to_apply=%region_34.35 | all-reduce | flops 5888 | bytes 47104 | tf_op jit(solution)/shard_map/psum | solution.py:640
  947.8 12.6 %collective-permute-done.42 = bf16[304,448]{0,1:T(8,128)(2,1)} collective-permute-done((bf16[304,448]{0,1:T(8,128)(2,1)}, bf16[304,448]{0,1:T(8,128)(2,1)}, u32[]{:S(2)}, u32[]{:S(2)}) %collective-permute-start.42) | collective-permute-done | bytes 272416 | tf_op jit(solution)/shard_map/ppermute | solution.py:485
  1063.6 9.9 collective-permute-done.26
  1073.6 21.7 %collective-permute-done.27 = bf16[56,4864]{1,0:T(8,128)(2,1)S(1)} collective-permute-done((bf16[56,4864]{1,0:T(8,128)(2,1)S(1)}, bf16[56,4864]{1,0:T(8,128)(2,1)S(1)}, u32[]{:S(2)}, u32[]{:S(2)}) %collective-permute-start.27) | collective-permute-done | bytes 544800 | tf_op jit(solution)/shard_map/ppermute | solution.py:485
  1102.9 12.2 %collective-permute-start.19 = (bf16[56,4864]{1,0:T(8,128)(2,1)S(1)}, bf16[56,4864]{1,0:T(8,128)(2,1)S(1)}, u32[]{:S(2)}, u32[]{:S(2)}) collective-permute-start(bf16[56,4864]{1,0:T(8,128)(2,1)S(1)} %get-tuple-element.73), channel_id=1, source_target_pairs={{0,4},{4,8},{8,12},{12,0},{1,5},{5,9},{9,13},{13,1},{2,6},{6,10},{... | collective-permute-start | bytes 1634312 | tf_op jit(solution)/shard_map/ppermute | solution.py:485
  1115.1 9.6 collective-permute-start.20
  1132.9 16.8 %collective-permute-done.20 = bf16[56,4864]{1,0:T(8,128)(2,1)S(1)} collective-permute-done((bf16[56,4864]{1,0:T(8,128)(2,1)S(1)}, bf16[56,4864]{1,0:T(8,128)(2,1)S(1)}, u32[]{:S(2)}, u32[]{:S(2)}) %collective-permute-start.20) | collective-permute-done | bytes 544800 | tf_op jit(solution)/shard_map/ppermute | solution.py:485
  1155.5 11.6 collective-permute-done.22
  1167.1 10.7 collective-permute-done.23
  (680 shorter events, 568.4 us)
Async XLA Ops:
  7.2 540.3 %reduce-scatter.9.cloned.1.call-start = ((), (), s32[]{:S(2)}) async-start(), calls=%async_computation.8 | async-start | bytes 655360 | tf_op jit(solution)/shard_map/reduce_scatter | solution.py:607
  8.5 339.5 %collective-permute-start = (bf16[256,896]{1,0:T(8,128)(2,1)S(1)}, bf16[256,896]{1,0:T(8,128)(2,1)S(1)}, u32[]{:S(2)}, u32[]{:S(2)}) collective-permute-start(bf16[256,896]{1,0:T(8,128)(2,1)S(1)} %bitcast_select_fusion.5), channel_id=1, source_target_pairs={{0,16},{16,0},{1,17},{17,1},{2,18},{18,2},{3,19},{19,3},{4,20},{20... | collective-permute-start | bytes 1376264 | tf_op jit(solution)/shard_map/ppermute | solution.py:476
  527.4 122.1 %reduce-scatter.11.cloned.1.call-start = ((), (), s32[]{:S(2)}) async-start(), calls=%async_computation.9 | async-start | bytes 655360 | tf_op jit(solution)/shard_map/reduce_scatter | solution.py:607
  630.0 235.0 %reduce-scatter.15.cloned.1.call-start = ((), (), s32[]{:S(2)}) async-start(), calls=%async_computation.11 | async-start | bytes 2293760 | tf_op jit(solution)/shard_map/reduce_scatter | solution.py:492
  640.6 277.6 %reduce-scatter.13.cloned.1.call-start = ((), (), s32[]{:S(2)}) async-start(), calls=%async_computation.10 | async-start | bytes 2293760 | tf_op jit(solution)/shard_map/reduce_scatter | solution.py:492
  678.3 32.7 %collective-permute-start.40 = (bf16[4864,448]{0,1:T(8,128)(2,1)}, bf16[4864,448]{0,1:T(8,128)(2,1)}, u32[]{:S(2)}, u32[]{:S(2)}) collective-permute-start(bf16[4864,448]{0,1:T(8,128)(2,1)} %copy.213), channel_id=1, source_target_pairs={{0,16},{16,0},{1,17},{17,1},{2,18},{18,2},{3,19},{19,3},{4,20},{20... | collective-permute-start | bytes 13074440 | tf_op jit(solution)/shard_map/ppermute | solution.py:476
  685.3 240.6 %reduce-scatter.23.cloned.1.call-start = ((), (), s32[]{:S(2)}) async-start(), calls=%async_computation.15 | async-start | bytes 6225920 | tf_op jit(solution)/shard_map/reduce_scatter | solution.py:492
  727.6 238.5 %reduce-scatter.21.cloned.1.call-start = ((), (), s32[]{:S(2)}) async-start(), calls=%async_computation.14 | async-start | bytes 6225920 | tf_op jit(solution)/shard_map/reduce_scatter | solution.py:492
  753.8 36.0 %collective-permute-start.33 = (bf16[4864,448]{0,1:T(8,128)(2,1)}, bf16[4864,448]{0,1:T(8,128)(2,1)}, u32[]{:S(2)}, u32[]{:S(2)}) collective-permute-start(bf16[4864,448]{0,1:T(8,128)(2,1)} %copy.203), channel_id=1, source_target_pairs={{0,16},{16,0},{1,17},{17,1},{2,18},{18,2},{3,19},{19,3},{4,20},{20... | collective-permute-start | bytes 13074440 | tf_op jit(solution)/shard_map/ppermute | solution.py:476
  764.9 41.7 %collective-permute-start.25 = (bf16[896,4864]{1,0:T(8,128)(2,1)}, bf16[896,4864]{1,0:T(8,128)(2,1)}, u32[]{:S(2)}, u32[]{:S(2)}) collective-permute-start(bf16[896,4864]{1,0:T(8,128)(2,1)} %convolution_convert_fusion), channel_id=1, source_target_pairs={{0,16},{16,0},{1,17},{17,1},{2,18},{18,2},{3,19},{19,3},{4,20},{20... | collective-permute-start | bytes 26148872 | tf_op jit(solution)/shard_map/ppermute | solution.py:476
  806.4 248.4 %reduce-scatter.19.cloned.1.call-start = ((), (), s32[]{:S(2)}) async-start(), calls=%async_computation.13 | async-start | bytes 10895360 | tf_op jit(solution)/shard_map/reduce_scatter | solution.py:492
  818.0 283.4 %reduce-scatter.17.cloned.1.call-start = ((), (), s32[]{:S(2)}) async-start(), calls=%async_computation.12 | async-start | bytes 10895360 | tf_op jit(solution)/shard_map/reduce_scatter | solution.py:492
  868.6 46.1 %collective-permute-start.11 = (bf16[28,2048]{1,0:T(8,128)(2,1)}, bf16[28,2048]{1,0:T(8,128)(2,1)S(1)}, u32[]{:S(2)}, u32[]{:S(2)}) collective-permute-start(bf16[28,2048]{1,0:T(8,128)(2,1)} %get-tuple-element.102), channel_id=1, source_target_pairs={{0,4},{4,8},{8,12},{12,0},{1,5},{5,9},{9,13},{13,1},{2,6},{6,10},{... | collective-permute-start | bytes 344072 | tf_op jit(solution)/shard_map/ppermute | solution.py:485
  868.6 46.1 %collective-permute-start.12 = (bf16[28,2048]{1,0:T(8,128)(2,1)}, bf16[28,2048]{1,0:T(8,128)(2,1)}, u32[]{:S(2)}, u32[]{:S(2)}) collective-permute-start(bf16[28,2048]{1,0:T(8,128)(2,1)} %get-tuple-element.104), channel_id=1, source_target_pairs={{0,8},{4,12},{8,0},{12,4},{1,9},{5,13},{9,1},{13,5},{2,10},{6,14},... | collective-permute-start | bytes 344072 | tf_op jit(solution)/shard_map/ppermute | solution.py:485
  870.3 44.4 %collective-permute-start.13 = (bf16[28,2048]{1,0:T(8,128)(2,1)S(1)}, bf16[28,2048]{1,0:T(8,128)(2,1)}, u32[]{:S(2)}, u32[]{:S(2)}) collective-permute-start(bf16[28,2048]{1,0:T(8,128)(2,1)S(1)} %get-tuple-element.103), channel_id=1, source_target_pairs={{0,12},{4,0},{8,4},{12,8},{1,13},{5,1},{9,5},{13,9},{2,14},{6,2},{... | collective-permute-start | bytes 344072 | tf_op jit(solution)/shard_map/ppermute | solution.py:485
  914.1 50.6 %collective-permute-start.2 = (f32[256,896]{1,0:T(8,128)}, f32[256,896]{1,0:T(8,128)}, u32[]{:S(2)}, u32[]{:S(2)}) collective-permute-start(f32[256,896]{1,0:T(8,128)} %broadcast_select_fusion.6), channel_id=1, source_target_pairs={{0,16},{16,0},{1,17},{17,1},{2,18},{18,2},{3,19},{19,3},{4,20},{20... | collective-permute-start | bytes 2752520 | tf_op jit(solution)/shard_map/ppermute | solution.py:476
  915.8 58.3 %collective-permute-start.14 = (bf16[28,2048]{1,0:T(8,128)(2,1)S(1)}, bf16[28,2048]{1,0:T(8,128)(2,1)}, u32[]{:S(2)}, u32[]{:S(2)}) collective-permute-start(bf16[28,2048]{1,0:T(8,128)(2,1)S(1)} %fusion.162), channel_id=1, source_target_pairs={{0,1},{1,0},{2,3},{3,2},{4,5},{5,4},{6,7},{7,6},{8,9},{9,8},{10,11... | collective-permute-start | bytes 344072 | tf_op jit(solution)/shard_map/ppermute | solution.py:501
  1007.7 36.5 %collective-permute-start.38 = (bf16[304,448]{0,1:T(8,128)(2,1)S(1)}, bf16[304,448]{0,1:T(8,128)(2,1)}, u32[]{:S(2)}, u32[]{:S(2)}) collective-permute-start(bf16[304,448]{0,1:T(8,128)(2,1)S(1)} %fusion.159), channel_id=1, source_target_pairs={{0,2},{1,3},{2,0},{3,1},{4,6},{5,7},{6,4},{7,5},{8,10},{9,11},{10,... | collective-permute-start | bytes 817160 | tf_op jit(solution)/shard_map/ppermute | solution.py:501
  1008.2 42.8 %collective-permute-start.39 = (bf16[304,448]{0,1:T(8,128)(2,1)S(1)}, bf16[304,448]{0,1:T(8,128)(2,1)S(1)}, u32[]{:S(2)}, u32[]{:S(2)}) collective-permute-start(bf16[304,448]{0,1:T(8,128)(2,1)S(1)} %fusion.159), channel_id=1, source_target_pairs={{0,3},{1,2},{2,1},{3,0},{4,7},{5,6},{6,5},{7,4},{8,11},{9,10},{10,... | collective-permute-start | bytes 817160 | tf_op jit(solution)/shard_map/ppermute | solution.py:501
  1025.8 155.4 %collective-permute-start.17 = (bf16[112,2048]{1,0:T(8,128)(2,1)}, bf16[112,2048]{1,0:T(8,128)(2,1)}, u32[]{:S(2)}, u32[]{:S(2)}) collective-permute-start(bf16[112,2048]{1,0:T(8,128)(2,1)} %broadcast_select_fusion.4), channel_id=1, source_target_pairs={{0,16},{16,0},{1,17},{17,1},{2,18},{18,2},{3,19},{19,3},{4,20},{20... | collective-permute-start | bytes 1376264 | tf_op jit(solution)/shard_map/ppermute | solution.py:476
  1058.1 37.2 %collective-permute-start.27 = (bf16[56,4864]{1,0:T(8,128)(2,1)S(1)}, bf16[56,4864]{1,0:T(8,128)(2,1)S(1)}, u32[]{:S(2)}, u32[]{:S(2)}) collective-permute-start(bf16[56,4864]{1,0:T(8,128)(2,1)S(1)} %get-tuple-element.78), channel_id=1, source_target_pairs={{0,8},{4,12},{8,0},{12,4},{1,9},{5,13},{9,1},{13,5},{2,10},{6,14},... | collective-permute-start | bytes 1634312 | tf_op jit(solution)/shard_map/ppermute | solution.py:485
  1059.7 35.6 %collective-permute-start.28 = (bf16[56,4864]{1,0:T(8,128)(2,1)S(1)}, bf16[56,4864]{1,0:T(8,128)(2,1)S(1)}, u32[]{:S(2)}, u32[]{:S(2)}) collective-permute-start(bf16[56,4864]{1,0:T(8,128)(2,1)S(1)} %get-tuple-element.77), channel_id=1, source_target_pairs={{0,12},{4,0},{8,4},{12,8},{1,13},{5,1},{9,5},{13,9},{2,14},{6,2},{... | collective-permute-start | bytes 1634312 | tf_op jit(solution)/shard_map/ppermute | solution.py:485
  1063.6 121.0 %collective-permute-start.47 = (bf16[1216,448]{0,1:T(8,128)(2,1)}, bf16[1216,448]{0,1:T(8,128)(2,1)}, u32[]{:S(2)}, u32[]{:S(2)}) collective-permute-start(bf16[1216,448]{0,1:T(8,128)(2,1)} %broadcast_select_fusion.2), channel_id=1, source_target_pairs={{0,16},{16,0},{1,17},{17,1},{2,18},{18,2},{3,19},{19,3},{4,20},{20... | collective-permute-start | bytes 3268616 | tf_op jit(solution)/shard_map/ppermute | solution.py:476
  1115.1 34.5 %collective-permute-start.20 = (bf16[56,4864]{1,0:T(8,128)(2,1)S(1)}, bf16[56,4864]{1,0:T(8,128)(2,1)S(1)}, u32[]{:S(2)}, u32[]{:S(2)}) collective-permute-start(bf16[56,4864]{1,0:T(8,128)(2,1)S(1)} %get-tuple-element.75), channel_id=1, source_target_pairs={{0,8},{4,12},{8,0},{12,4},{1,9},{5,13},{9,1},{13,5},{2,10},{6,14},... | collective-permute-start | bytes 1634312 | tf_op jit(solution)/shard_map/ppermute | solution.py:485
  (180 other events, 2049.4 us)
Sparse Core Ops, SparseCore 0:
  527.5 19.0 reduce-scatter.8
  630.1 19.2 reduce-scatter.10
  653.1 31.2 reduce-scatter.14
  687.3 32.9 reduce-scatter.12
  727.7 57.4 reduce-scatter.22
  806.5 57.5 reduce-scatter.20
  867.2 95.9 reduce-scatter.18
  966.3 121.3 reduce-scatter.16
